TPU v7x, 32 devices: a whole 2x2x4 slice. The times are simulated.
32 devices in a mesh: dp: 16 (over z, y, x), tensor: 2 (over core).
Axes of the slice: x: 2, y: 2, z: 4, core: 2. Of those that a mesh axis runs over, the one named last changes fastest.
Arguments:
- tokens: bfloat16 [4096, 768], P('dp'), may hold values from -6 to 6
- cotangent: bfloat16 [4096, 768], P('dp'), may hold values from -6 to 6
- attn_gain: float32 [768], P('dp'), may hold values from 0.5 to 1.5
- w_query: float32 [768, 768], P('dp', 'tensor'), may hold values from -0.21875 to 0.21875
- w_key: float32 [768, 768], P('dp', 'tensor'), may hold values from -0.21875 to 0.21875
- w_value: float32 [768, 768], P('dp', 'tensor'), may hold values from -0.21875 to 0.21875
- w_out: float32 [768, 768], P('tensor', 'dp'), may hold values from -0.875 to 0.875
- ffn_gain: float32 [768], P('dp'), may hold values from 0.5 to 1.5
- w_router: float32 [768, 16], P('dp'), may hold values from -0.15625 to 0.15625
- w_sgate: float32 [768, 2048], P('dp', 'tensor'), may hold values from -0.21875 to 0.21875
- w_sup: float32 [768, 2048], P('dp', 'tensor'), may hold values from -0.21875 to 0.21875
- w_sdown: float32 [2048, 768], P('tensor', 'dp'), may hold values from -0.125 to 0.125
- e_gate: float32 [768, 32768], P(None, ('dp', 'tensor')), may hold values from -0.21875 to 0.21875
- e_up: float32 [768, 32768], P(None, ('dp', 'tensor')), may hold values from -0.21875 to 0.21875
- e_down: float32 [32768, 768], P(('dp', 'tensor')), may hold values from -2 to 2
- routes: int32 [4096, 2], P('dp'), may hold values from 0 to 15, all different within a row; in each aligned block of 256 rows (0 to 255, 256 to 511, ...) at most 64 rows name the same one
- segments: int32 [4096], replicated, may hold values from 0 to 15, never falling along the last dimension, each value on 1 to 2048 neighbouring positions
Outputs:
- output: bfloat16 [4096, 768], P('dp')
- token_input_gradient: float32 [4096, 768], P('dp')
- grad_attn_gain: float32 [768], P('dp')
- grad_w_query: float32 [768, 768], P('dp', 'tensor')
- grad_w_key: float32 [768, 768], P('dp', 'tensor')
- grad_w_value: float32 [768, 768], P('dp', 'tensor')
- grad_w_out: float32 [768, 768], P('tensor', 'dp')
- grad_ffn_gain: float32 [768], P('dp')
- grad_w_router: float32 [768, 16], P('dp')
- grad_w_sgate: float32 [768, 2048], P('dp', 'tensor')
- grad_w_sup: float32 [768, 2048], P('dp', 'tensor')
- grad_w_sdown: float32 [2048, 768], P('tensor', 'dp')
- grad_e_gate: float32 [768, 32768], P(None, ('dp', 'tensor'))
- grad_e_up: float32 [768, 32768], P(None, ('dp', 'tensor'))
- grad_e_down: float32 [32768, 768], P(('dp', 'tensor'))
Inputs may be any that keep to these rules, and one draw needn't show every extreme that they name: `routes`: the 2 experts of a token differ. Among the 256 rows of one index of dp, no expert is named by more than 64 rows, and in every draw some expert is named by exactly 64 rows of some index. `segments`: document numbers never fall along the tokens; each document holds 1 to 2048 tokens, and one holds exactly 2048.
All inputs are finite; a program needn't handle non-finite values.
Results may differ from a plain program's by a relative error of at most 0.024.
Values may be sent and summed in bfloat16 or wider, within the bound.
A program may use at most 256 MiB of HBM per device.

v0:
```python
import jax
import jax.numpy as jnp
from jax import lax
from jax.sharding import PartitionSpec as P

HEAD = 64
WINDOW = 1024


eps = 1e-06
masked = -1e30


def passed_along(value, axis, by):
    devices = lax.axis_size(axis)
    pairs = [(i, i + by) for i in range(devices) if 0 <= i + by < devices]
    return lax.ppermute(value, axis, pairs)


def matmul(left, right):
    return jnp.dot(left, right, preferred_element_type=jnp.float32)


def weight_grad(left, right):
    return lax.dot_general(
        left, right, (((0,), (0,)), ((), ())), preferred_element_type=jnp.float32
    )


def input_grad(left, right):
    return lax.dot_general(
        left, right, (((1,), (1,)), ((), ())), preferred_element_type=jnp.float32
    )


def rms_parts(values):
    factor = lax.rsqrt(jnp.mean(values * values, axis=-1, keepdims=True) + eps)
    return (values * factor, factor)


def rotary_tables(positions):
    freqs = 10000.0 ** (-jnp.arange(HEAD // 2, dtype=jnp.float32) * (2.0 / HEAD))
    phase = positions.astype(jnp.float32)[:, None] * freqs[None, :]
    return (jnp.cos(phase)[:, None, :], jnp.sin(phase)[:, None, :])


def rotate(values, cosines, sines):
    half = values.shape[-1] // 2
    first = values[..., :half]
    second = values[..., half:]
    return jnp.concatenate(
        [first * cosines - second * sines, second * cosines + first * sines], axis=-1
    )


def unrotate(grads, cosines, sines):
    half = grads.shape[-1] // 2
    first = grads[..., :half]
    second = grads[..., half:]
    return jnp.concatenate(
        [first * cosines + second * sines, second * cosines - first * sines], axis=-1
    )


def silu_grad(values):
    sigma = jax.nn.sigmoid(values)
    return sigma * (1.0 + values * (1.0 - sigma))


def masked_scores(queries, keys, valid):
    scores = jnp.einsum("qhe,khe->hqk", queries, keys, preferred_element_type=jnp.float32)
    return jnp.where(valid[None, :, :], scores, masked)


def local(
    tokens,
    cotangent,
    attn_gain,
    w_query,
    w_key,
    w_value,
    w_out,
    ffn_gain,
    w_router,
    w_sgate,
    w_sup,
    w_sdown,
    e_gate,
    e_up,
    e_down,
    routes,
    segments,
):
    tok_count, width = tokens.shape
    dp_count = lax.axis_size("dp")
    dp_place = lax.axis_index("dp")
    experts = w_router.shape[1]
    owners = dp_count // experts
    capacity = tok_count // 4
    reach = (WINDOW + tok_count - 1) // tok_count
    score_scale = HEAD ** (-0.5)
    gathered = (
        lax.all_gather(attn_gain.astype(jnp.bfloat16), "dp", axis=0, tiled=True),
        lax.all_gather(w_query.astype(jnp.bfloat16), "dp", axis=0, tiled=True),
        lax.all_gather(w_key.astype(jnp.bfloat16), "dp", axis=0, tiled=True),
        lax.all_gather(w_value.astype(jnp.bfloat16), "dp", axis=0, tiled=True),
        lax.all_gather(w_out.astype(jnp.bfloat16), "dp", axis=1, tiled=True),
        lax.all_gather(ffn_gain.astype(jnp.bfloat16), "dp", axis=0, tiled=True),
        lax.all_gather(w_router.astype(jnp.bfloat16), "dp", axis=0, tiled=True),
        lax.all_gather(w_sgate.astype(jnp.bfloat16), "dp", axis=0, tiled=True),
        lax.all_gather(w_sup.astype(jnp.bfloat16), "dp", axis=0, tiled=True),
        lax.all_gather(w_sdown.astype(jnp.bfloat16), "dp", axis=1, tiled=True),
    )
    gain_one, query_w, key_w, value_w, out_w, gain_two, router_w, sgate_w, sup_w, sdown_w = gathered
    expert_gate = e_gate.astype(jnp.bfloat16)
    expert_up = e_up.astype(jnp.bfloat16)
    expert_down = e_down.astype(jnp.bfloat16)
    local_heads = query_w.shape[1] // HEAD
    head_shape = (tok_count, local_heads, HEAD)
    token_rows = dp_place * tok_count + jnp.arange(tok_count, dtype=jnp.int32)
    cosines, sines = rotary_tables(token_rows)
    key_rows = (dp_place - reach) * tok_count + jnp.arange((reach + 1) * tok_count, dtype=jnp.int32)
    seg_query = segments[token_rows]
    seg_key = segments[jnp.maximum(key_rows, 0)]
    later = token_rows[:, None]
    earlier = key_rows[None, :]
    valid = (earlier >= 0) & (earlier <= later) & (later - earlier < WINDOW)
    valid = valid & (seg_key[None, :] == seg_query[:, None])
    x_float = tokens.astype(jnp.float32)
    normed_one, scale_one = rms_parts(x_float)
    gain_first = gain_one.astype(jnp.float32)
    attn_in = (normed_one * gain_first).astype(jnp.bfloat16)
    queries = (
        rotate(matmul(attn_in, query_w).reshape(head_shape), cosines, sines) * score_scale
    ).astype(jnp.bfloat16)
    keys_own = (
        rotate(matmul(attn_in, key_w).reshape(head_shape), cosines, sines)
        .astype(jnp.bfloat16)
        .reshape(tok_count, -1)
    )
    values_own = matmul(attn_in, value_w).astype(jnp.bfloat16)
    key_list = [keys_own]
    value_list = [values_own]
    for offset in range(1, reach + 1):
        far_keys, far_values = passed_along((keys_own, values_own), "dp", offset)
        key_list.insert(0, far_keys)
        value_list.insert(0, far_values)
    all_keys = jnp.concatenate(key_list, axis=0).reshape(-1, local_heads, HEAD)
    all_values = jnp.concatenate(value_list, axis=0).reshape(-1, local_heads, HEAD)
    scores = masked_scores(queries, all_keys, valid)
    peak = jnp.max(scores, axis=-1, keepdims=True)
    lse = peak + jnp.log(jnp.sum(jnp.exp(scores - peak), axis=-1, keepdims=True))
    weights = jnp.exp(scores - lse)
    heads_out = (
        jnp.einsum(
            "hqk,khe->qhe",
            weights.astype(jnp.bfloat16),
            all_values,
            preferred_element_type=jnp.float32,
        )
        .astype(jnp.bfloat16)
        .reshape(tok_count, -1)
    )
    middle = x_float + lax.psum(matmul(heads_out, out_w).astype(jnp.bfloat16), "tensor").astype(
        jnp.float32
    )
    normed_two, scale_two = rms_parts(middle)
    gain_second = gain_two.astype(jnp.float32)
    branch_in = (normed_two * gain_second).astype(jnp.bfloat16)
    logits = matmul(branch_in, router_w)
    expo = jnp.exp(logits - jnp.max(logits, axis=-1, keepdims=True))
    probs = expo / jnp.sum(expo, axis=-1, keepdims=True)
    picked = (routes[:, :, None] == jnp.arange(experts, dtype=jnp.int32)[None, None, :]).astype(
        jnp.float32
    )
    gates = jnp.sum(probs[:, None, :] * picked, axis=2)
    chosen = jnp.sum(picked, axis=1)
    before = jnp.cumsum(chosen, axis=0) - chosen
    slot_ids = jnp.arange(capacity, dtype=jnp.float32)
    taken = (before.T[:, None, :] == slot_ids[None, :, None]) & (chosen.T[:, None, :] > 0.5)
    alive = jnp.any(taken, axis=2)
    source_rows = jnp.sum(
        jnp.where(taken, jnp.arange(tok_count, dtype=jnp.int32)[None, None, :], 0), axis=2
    )
    pair_slot = routes * capacity + jnp.sum(picked * before[:, None, :], axis=2).astype(jnp.int32)
    gate_slot = jnp.where(alive, jnp.take_along_axis((probs * chosen).T, source_rows, axis=1), 0.0)
    shared_gate = matmul(branch_in, sgate_w)
    shared_up = matmul(branch_in, sup_w)
    shared_act = jax.nn.silu(shared_gate)
    shared_hidden = (shared_act * shared_up).astype(jnp.bfloat16)
    shared_part = matmul(shared_hidden, sdown_w)

    def outgoing(rows):
        return jnp.repeat(rows, owners, axis=0)

    def incoming(rows):
        return jnp.sum(
            rows.reshape(experts, owners, capacity, width).astype(jnp.float32), axis=1
        ).reshape(experts * capacity, width)

    dispatched = jnp.where(alive[:, :, None], branch_in[source_rows], jnp.zeros((), jnp.bfloat16))
    received_rows = lax.all_to_all(
        outgoing(dispatched), "dp", split_axis=0, concat_axis=0, tiled=True
    )
    gate_hidden = jnp.einsum(
        "scd,dh->sch", received_rows, expert_gate, preferred_element_type=jnp.float32
    )
    up_hidden = jnp.einsum(
        "scd,dh->sch", received_rows, expert_up, preferred_element_type=jnp.float32
    )
    hidden = (jax.nn.silu(gate_hidden) * up_hidden).astype(jnp.bfloat16)
    partial_rows = jnp.einsum(
        "sch,hd->scd", hidden, expert_down, preferred_element_type=jnp.float32
    ).astype(jnp.bfloat16)
    returned = lax.all_to_all(partial_rows, "dp", split_axis=0, concat_axis=0, tiled=True)
    returned, received_rows, gate_hidden, up_hidden = (
        returned,
        received_rows,
        gate_hidden,
        up_hidden,
    )
    pair_out = incoming(returned)[pair_slot]
    moe_part = jnp.sum(gates[:, :, None] * pair_out, axis=1)
    after = middle + lax.psum((moe_part + shared_part).astype(jnp.bfloat16), "tensor").astype(
        jnp.float32
    )
    output = after.astype(jnp.bfloat16)
    d_after = cotangent.astype(jnp.float32)
    d_shared = input_grad(cotangent, sdown_w)
    grad_sdown = weight_grad(shared_hidden, cotangent)
    d_sgate = (d_shared * shared_up * silu_grad(shared_gate)).astype(jnp.bfloat16)
    d_sup = (d_shared * shared_act).astype(jnp.bfloat16)
    grad_sgate = weight_grad(branch_in, d_sgate)
    grad_sup = weight_grad(branch_in, d_sup)
    d_shared_in = input_grad(d_sgate, sgate_w) + input_grad(d_sup, sup_w)
    d_rows = jnp.where(alive[:, :, None], gate_slot[:, :, None] * d_after[source_rows], 0.0).astype(
        jnp.bfloat16
    )
    d_arrived = lax.all_to_all(outgoing(d_rows), "dp", split_axis=0, concat_axis=0, tiled=True)
    gate_act = jax.nn.silu(gate_hidden)
    hidden = (gate_act * up_hidden).astype(jnp.bfloat16)
    d_hidden = jnp.einsum("scd,hd->sch", d_arrived, expert_down, preferred_element_type=jnp.float32)
    expert_down_gradient = jnp.einsum(
        "sch,scd->hd", hidden, d_arrived, preferred_element_type=jnp.float32
    )
    d_gate_hidden = (d_hidden * up_hidden * silu_grad(gate_hidden)).astype(jnp.bfloat16)
    up_hidden_gradient = (d_hidden * gate_act).astype(jnp.bfloat16)
    expert_gate_gradient = jnp.einsum(
        "fen,feq->nq", received_rows, d_gate_hidden, preferred_element_type=jnp.float32
    )
    expert_up_gradient = jnp.einsum(
        "fen,feq->nq", received_rows, up_hidden_gradient, preferred_element_type=jnp.float32
    )
    d_expert_rows = (
        jnp.einsum("sch,dh->scd", d_gate_hidden, expert_gate, preferred_element_type=jnp.float32)
        + jnp.einsum(
            "sch,dh->scd", up_hidden_gradient, expert_up, preferred_element_type=jnp.float32
        )
    ).astype(jnp.bfloat16)
    d_returned = lax.all_to_all(d_expert_rows, "dp", split_axis=0, concat_axis=0, tiled=True)
    d_pairs = incoming(d_returned)[pair_slot]
    d_gates_part = jnp.sum(d_after[:, None, :] * pair_out, axis=2)
    d_branch_sum, d_gates = (
        lax.psum((d_shared_in + jnp.sum(d_pairs, axis=1)).astype(jnp.bfloat16), "tensor").astype(
            jnp.float32
        ),
        lax.psum(d_gates_part.astype(jnp.bfloat16), "tensor").astype(jnp.float32),
    )
    d_probs = jnp.sum(d_gates[:, :, None] * picked, axis=1)
    d_logits = (probs * (d_probs - jnp.sum(probs * d_probs, axis=-1, keepdims=True))).astype(
        jnp.bfloat16
    )
    grad_router = weight_grad(branch_in, d_logits)
    d_branch_in = d_branch_sum + input_grad(d_logits, router_w)
    grad_gain_two = jnp.sum(d_branch_in * normed_two, axis=0)
    d_norm_two = d_branch_in * gain_second
    d_middle = d_after + scale_two * (
        d_norm_two - normed_two * jnp.mean(d_norm_two * normed_two, axis=-1, keepdims=True)
    )
    d_attn = d_middle.astype(jnp.bfloat16)
    grad_out = weight_grad(heads_out, d_attn)
    d_heads = input_grad(d_attn, out_w).astype(jnp.bfloat16).reshape(head_shape)
    again = jnp.exp(masked_scores(queries, all_keys, valid) - lse)
    d_weights = jnp.einsum("qhe,khe->hqk", d_heads, all_values, preferred_element_type=jnp.float32)
    d_scores = (again * (d_weights - jnp.sum(again * d_weights, axis=-1, keepdims=True))).astype(
        jnp.bfloat16
    )
    d_queries = (
        jnp.einsum("hqk,khe->qhe", d_scores, all_keys, preferred_element_type=jnp.float32)
        * score_scale
    )
    d_keys_all = jnp.einsum(
        "hqk,qhe->khe", d_scores, queries, preferred_element_type=jnp.float32
    ).reshape(reach + 1, tok_count, -1)
    d_values_all = jnp.einsum(
        "hqk,qhe->khe", again.astype(jnp.bfloat16), d_heads, preferred_element_type=jnp.float32
    ).reshape(reach + 1, tok_count, -1)
    d_keys = d_keys_all[reach]
    d_values = d_values_all[reach]
    for offset in range(1, reach + 1):
        back_keys, back_values = (
            passed_along(d_keys_all[reach - offset].astype(jnp.bfloat16), "dp", -offset).astype(
                jnp.float32
            ),
            passed_along(d_values_all[reach - offset].astype(jnp.bfloat16), "dp", -offset).astype(
                jnp.float32
            ),
        )
        d_keys = d_keys + back_keys
        d_values = d_values + back_values
    d_query_pre = unrotate(d_queries, cosines, sines).astype(jnp.bfloat16).reshape(tok_count, -1)
    d_key_pre = (
        unrotate(d_keys.reshape(head_shape), cosines, sines)
        .astype(jnp.bfloat16)
        .reshape(tok_count, -1)
    )
    d_value_pre = d_values.astype(jnp.bfloat16)
    grad_query = weight_grad(attn_in, d_query_pre)
    grad_key = weight_grad(attn_in, d_key_pre)
    grad_value = weight_grad(attn_in, d_value_pre)
    d_attn_part = (
        input_grad(d_query_pre, query_w)
        + input_grad(d_key_pre, key_w)
        + input_grad(d_value_pre, value_w)
    )
    d_attn_in = lax.psum(d_attn_part.astype(jnp.bfloat16), "tensor").astype(jnp.float32)
    grad_gain_one = jnp.sum(d_attn_in * normed_one, axis=0)
    d_norm_one = d_attn_in * gain_first
    token_input_gradient = d_middle + scale_one * (
        d_norm_one - normed_one * jnp.mean(d_norm_one * normed_one, axis=-1, keepdims=True)
    )
    total_rows = (
        lax.psum_scatter(grad_gain_one, "dp", scatter_dimension=0, tiled=True),
        lax.psum_scatter(grad_query, "dp", scatter_dimension=0, tiled=True),
        lax.psum_scatter(grad_key, "dp", scatter_dimension=0, tiled=True),
        lax.psum_scatter(grad_value, "dp", scatter_dimension=0, tiled=True),
        lax.psum_scatter(grad_out, "dp", scatter_dimension=1, tiled=True),
        lax.psum_scatter(grad_gain_two, "dp", scatter_dimension=0, tiled=True),
        lax.psum_scatter(grad_router, "dp", scatter_dimension=0, tiled=True),
        lax.psum_scatter(grad_sgate, "dp", scatter_dimension=0, tiled=True),
        lax.psum_scatter(grad_sup, "dp", scatter_dimension=0, tiled=True),
        lax.psum_scatter(grad_sdown, "dp", scatter_dimension=1, tiled=True),
    )
    return (
        (output, token_input_gradient)
        + tuple(total_rows)
        + (expert_gate_gradient, expert_up_gradient, expert_down_gradient)
    )


def solution(mesh):
    in_specs = (
        P("dp", None),
        P("dp", None),
        P("dp"),
        P("dp", "tensor"),
        P("dp", "tensor"),
        P("dp", "tensor"),
        P("tensor", "dp"),
        P("dp"),
        P("dp", None),
        P("dp", "tensor"),
        P("dp", "tensor"),
        P("tensor", "dp"),
        P(None, ("dp", "tensor")),
        P(None, ("dp", "tensor")),
        P(("dp", "tensor"), None),
        P("dp", None),
        P(),
    )
    out_specs = (
        P("dp", None),
        P("dp", None),
        P("dp"),
        P("dp", "tensor"),
        P("dp", "tensor"),
        P("dp", "tensor"),
        P("tensor", "dp"),
        P("dp"),
        P("dp", None),
        P("dp", "tensor"),
        P("dp", "tensor"),
        P("tensor", "dp"),
        P(None, ("dp", "tensor")),
        P(None, ("dp", "tensor")),
        P(("dp", "tensor"), None),
    )
    return jax.shard_map(local, mesh=mesh, in_specs=in_specs, out_specs=out_specs, check_vma=False)
```

profile of v0, /device:TPU:0, one launch (start us, length us, event | category | flops | bytes accessed | tf_op | source)
XLA Modules:
  0.0 1622.3 jit_solution(6123643654210434853)
XLA Ops:
  9.0 45.7 %all_gather.31 = bf16[768,384]{1,0:T(8,128)(2,1)S(1)} all-gather(bf16[48,384]{1,0:T(8,128)(2,1)S(1)} %convert_element_type.244), channel_id=1, replica_groups=mesh['dp'=16,'tensor'=2] {'dp'}, dimensions={0}, use_global_device_ids=true | all-gather | bytes 626688 | tf_op jit(solution)/shard_map/all_gather | solution.py:106
  58.4 36.7 %all-reduce.5 = (bf16[768]{0:T(1024)(128)(2,1)S(1)}, bf16[768]{0:T(1024)(128)(2,1)S(1)}) all-reduce(bf16[768]{0:T(1024)(128)(2,1)S(1)} %dynamic-update-slice, bf16[768]{0:T(1024)(128)(2,1)S(1)} %dynamic-update-slice.1), channel_id=1, replica_groups=mesh['dp'=16,'tensor'=2] {'dp'}, use_global_device_ids=true, to_apply=%add | all-reduce | flops 1536 | bytes 6144
  101.7 3.8 collective-permute-start.3
  105.6 40.3 %all_gather.33 = bf16[768,384]{1,0:T(8,128)(2,1)S(1)} all-gather(bf16[48,384]{1,0:T(8,128)(2,1)S(1)} %convert_element_type.249), channel_id=1, replica_groups=mesh['dp'=16,'tensor'=2] {'dp'}, dimensions={0}, use_global_device_ids=true | all-gather | bytes 626688 | tf_op jit(solution)/shard_map/all_gather | solution.py:105
  149.6 7.1 gather_fusion
  158.5 40.6 %all_gather.32 = bf16[768,384]{1,0:T(8,128)(2,1)S(1)} all-gather(bf16[48,384]{1,0:T(8,128)(2,1)S(1)} %convert_element_type.246), channel_id=1, replica_groups=mesh['dp'=16,'tensor'=2] {'dp'}, dimensions={0}, use_global_device_ids=true | all-gather | bytes 626688 | tf_op jit(solution)/shard_map/all_gather | solution.py:104
  199.7 39.2 %all_gather.34 = bf16[384,768]{0,1:T(8,128)(2,1)S(1)} all-gather(bf16[384,48]{0,1:T(8,128)(2,1)S(1)} %convert_element_type.255), channel_id=1, replica_groups=mesh['dp'=16,'tensor'=2] {'dp'}, dimensions={1}, use_global_device_ids=true | all-gather | bytes 626688 | tf_op jit(solution)/shard_map/all_gather | solution.py:107
  244.8 4.1 collective-permute-start.7
  265.4 35.8 %all-gather = bf16[16,48,16]{1,2,0:T(8,128)(2,1)S(1)} all-gather(bf16[1,48,16]{1,2,0:T(8,128)(2,1)S(1)} %convert_bitcast_fusion), channel_id=1, replica_groups=mesh['dp'=16,'tensor'=2] {'dp'}, dimensions={0}, use_global_device_ids=true | all-gather | bytes 26112 | tf_op jit(solution)/shard_map/all_gather | solution.py:109
  306.4 4.0 gather_fusion.2
  311.7 3.8 all-to-all-start
  316.9 5.2 gather_fusion.4
  322.2 8.6 gather_fusion.6
  330.8 3.4 select_convert_fusion
  334.2 13.8 all-to-all-done
  348.1 9.6 all-to-all-start.2
  358.4 5.8 fusion.10
  364.2 3.8 fusion.6
  368.0 10.7 all-to-all-done.2
  378.7 10.2 multiply_convert_fusion.1
  393.2 26.6 %all-to-all-start.1 = ((bf16[16,64,768]{2,1,0:T(8,128)(2,1)}), bf16[16,64,768]{2,1,0:T(8,128)(2,1)S(1)}, u32[]{:S(2)}, u32[]{:S(2)}) async-start(bf16[16,64,768]{2,1,0:T(8,128)(2,1)} %convolution_convert_fusion), calls=%async_computation.1 | async-start | bytes 3145728 | tf_op jit(solution)/shard_map/all_to_all | solution.py:215
  420.6 4.5 fusion.8
  428.1 23.9 %all-to-all-done.1 = bf16[16,64,768]{2,1,0:T(8,128)(2,1)S(1)} async-done(((bf16[16,64,768]{2,1,0:T(8,128)(2,1)}), bf16[16,64,768]{2,1,0:T(8,128)(2,1)S(1)}, u32[]{:S(2)}, u32[]{:S(2)}) %all-to-all-start.1) | async-done | bytes 1572896 | tf_op jit(solution)/shard_map/all_to_all | solution.py:215
  451.9 6.3 all-to-all-start.3
  462.0 9.5 all-gather.7.cloned.1.call-done
  471.5 3.0 fusion.85
  474.6 57.2 %all-gather.9.cloned.1.call-done = bf16[1024,768]{0,1:T(8,128)(2,1)} async-done(((bf16[1024,48]{0,1:T(8,128)(2,1)}), bf16[1024,768]{0,1:T(8,128)(2,1)}) %all-gather.9.cloned.1.call-update) | async-done | bytes 1572880 | tf_op jit(solution)/shard_map/all_gather | solution.py:112
  531.7 3.9 multiply_convert_fusion.4
  540.0 5.1 gather_fusion.3
  547.3 3.9 multiply_reduce_fusion.1
  568.4 3.0 fusion.15
  571.4 12.7 all-reduce.13.cloned.1.call-done
  587.2 5.4 multiply_reduce_fusion
  592.5 5.2 fusion.83
  597.7 4.4 multiply_convert_fusion
  622.2 9.2 collective-permute-done.15
  651.4 5.2 convolution_bitcast_fusion.4
  656.6 3.5 convolution_bitcast_fusion.3
  660.1 5.0 convolution_bitcast_fusion.2
  665.1 30.0 %reduce-scatter.25.cloned.1.call-done = f32[48,16]{1,0:T(8,128)} async-done(((f32[768,16]{1,0:T(8,128)}), f32[48,16]{1,0:T(8,128)}) %reduce-scatter.25.cloned.1.call-update) | async-done | bytes 3088
  698.0 40.8 %all-reduce.4 = (f32[768]{0:T(1024)S(1)}, f32[768]{0:T(1024)S(1)}) all-reduce(f32[768]{0:T(1024)S(1)} %get-tuple-element.19, f32[768]{0:T(1024)S(1)} %copy-done.76), channel_id=2, replica_groups=mesh['dp'=16,'tensor'=2] {'dp'}, use_global_device_ids=true, to_apply=%region_27.28.clone | all-reduce | flops 1536 | bytes 12288
  742.4 88.5 %reduce-scatter.19.cloned.1.call-done = f32[48,1024]{1,0:T(8,128)} async-done(((f32[768,1024]{1,0:T(8,128)}), f32[48,1024]{1,0:T(8,128)}) %reduce-scatter.19.cloned.1.call-update) | async-done | bytes 196624 | tf_op jit(solution)/shard_map/reduce_scatter | solution.py:340
  830.9 135.8 %reduce-scatter.21.cloned.1.call-done = f32[48,1024]{1,0:T(8,128)} async-done(((f32[768,1024]{1,0:T(8,128)}), f32[48,1024]{1,0:T(8,128)}) %reduce-scatter.21.cloned.1.call-update) | async-done | bytes 196624 | tf_op jit(solution)/shard_map/reduce_scatter | solution.py:341
  966.7 135.2 %reduce-scatter.23.cloned.1.call-done = f32[1024,48]{0,1:T(8,128)} async-done(((f32[1024,768]{0,1:T(8,128)}), f32[1024,48]{0,1:T(8,128)}) %reduce-scatter.23.cloned.1.call-update) | async-done | bytes 196624 | tf_op jit(solution)/shard_map/reduce_scatter | solution.py:342
  1102.0 128.1 %reduce-scatter.17.cloned.1.call-done = f32[384,48]{0,1:T(8,128)} async-done(((f32[384,768]{0,1:T(8,128)}), f32[384,48]{0,1:T(8,128)}) %reduce-scatter.17.cloned.1.call-update) | async-done | bytes 73744 | tf_op jit(solution)/shard_map/reduce_scatter | solution.py:337
  1230.0 128.1 %reduce-scatter.11.cloned.1.call-done = f32[48,384]{1,0:T(8,128)} async-done(((f32[768,384]{1,0:T(8,128)}), f32[48,384]{1,0:T(8,128)}) %reduce-scatter.11.cloned.1.call-update) | async-done | bytes 73744 | tf_op jit(solution)/shard_map/reduce_scatter | solution.py:334
  1358.1 128.3 %reduce-scatter.13.cloned.1.call-done = f32[48,384]{1,0:T(8,128)} async-done(((f32[768,384]{1,0:T(8,128)}), f32[48,384]{1,0:T(8,128)}) %reduce-scatter.13.cloned.1.call-update) | async-done | bytes 73744 | tf_op jit(solution)/shard_map/reduce_scatter | solution.py:335
  1486.4 128.1 %reduce-scatter.15.cloned.1.call-done = f32[48,384]{1,0:T(8,128)} async-done(((f32[768,384]{1,0:T(8,128)}), f32[48,384]{1,0:T(8,128)}) %reduce-scatter.15.cloned.1.call-update) | async-done | bytes 73744 | tf_op jit(solution)/shard_map/reduce_scatter | solution.py:336
  (361 shorter events, 130.7 us)
Async XLA Ops:
  8.0 141.6 %copy-start = (s32[4096]{0:T(1024)S(1)}, s32[4096]{0:T(1024)}, u32[]{:S(2)}) copy-start(s32[4096]{0:T(1024)} %param.33) | copy-start | bytes 49156
  8.0 138.7 %copy-start.3 = (bf16[256,768]{1,0:T(8,128)(2,1)S(1)}, bf16[256,768]{1,0:T(8,128)(2,1)}, u32[]{:S(2)}) copy-start(bf16[256,768]{1,0:T(8,128)(2,1)} %param.17) | copy-start | bytes 1179652
  8.0 97.5 %copy-start.64 = (f32[48,384]{1,0:T(8,128)S(1)}, f32[48,384]{1,0:T(8,128)}, u32[]{:S(2)}) copy-start(f32[48,384]{1,0:T(8,128)} %param.21) | copy-start | bytes 221188
  8.1 294.1 %all-reduce.11.cloned.1.call-start = ((), (), s32[]{:S(2)}) async-start(), calls=%async_computation.12 | async-start | bytes 786432 | tf_op jit(solution)/shard_map/psum | solution.py:164
  54.7 92.7 %copy-start.26 = (bf16[768,384]{1,0:T(8,128)(2,1)}, bf16[768,384]{1,0:T(8,128)(2,1)S(1)}, u32[]{:S(2)}) copy-start(bf16[768,384]{1,0:T(8,128)(2,1)S(1)} %all_gather.31) | copy-start | bytes 1769476
  95.2 103.9 %copy-start.52 = (f32[768]{0:T(1024)}, f32[768]{0:T(1024)S(1)}, u32[]{:S(2)}) copy-start(f32[768]{0:T(1024)S(1)} %convert_element_type.242) | copy-start | bytes 9220
  96.4 102.7 %copy-start.67 = (f32[256]{0:T(256)}, f32[256]{0:T(256)S(1)}, u32[]{:S(2)}) copy-start(f32[256]{0:T(256)S(1)} %add_rsqrt_fusion.1) | copy-start | bytes 3076
  97.8 141.6 %collective-permute-start = (bf16[256,384]{1,0:T(8,128)(2,1)S(1)}, bf16[256,384]{1,0:T(8,128)(2,1)S(1)}, u32[]{:S(2)}, u32[]{:S(2)}) collective-permute-start(bf16[256,384]{1,0:T(8,128)(2,1)S(1)} %convolution_convert_fusion.4), channel_id=1, source_target_pairs={{0,8},{2,10},{4,12},{6,14},{8,16},{10,18},{12,20},{14,22},{16,24},... | collective-permute-start | bytes 589832 | tf_op jit(solution)/shard_map/ppermute | solution.py:17
  99.1 143.0 %collective-permute-start.1 = (bf16[256,384]{1,0:T(8,128)(2,1)S(1)}, bf16[256,384]{1,0:T(8,128)(2,1)S(1)}, u32[]{:S(2)}, u32[]{:S(2)}) collective-permute-start(bf16[256,384]{1,0:T(8,128)(2,1)S(1)} %convolution_convert_fusion.4), channel_id=1, source_target_pairs={{0,6},{2,8},{4,10},{6,12},{8,14},{10,16},{12,18},{14,20},{16,22},{... | collective-permute-start | bytes 589832 | tf_op jit(solution)/shard_map/ppermute | solution.py:17
  100.4 144.4 %collective-permute-start.2 = (bf16[256,384]{1,0:T(8,128)(2,1)S(1)}, bf16[256,384]{1,0:T(8,128)(2,1)S(1)}, u32[]{:S(2)}, u32[]{:S(2)}) collective-permute-start(bf16[256,384]{1,0:T(8,128)(2,1)S(1)} %convolution_convert_fusion.4), channel_id=1, source_target_pairs={{0,4},{2,6},{4,8},{6,10},{8,12},{10,14},{12,16},{14,18},{16,20},{1... | collective-permute-start | bytes 589832 | tf_op jit(solution)/shard_map/ppermute | solution.py:17
  101.7 147.9 %collective-permute-start.3 = (bf16[256,384]{1,0:T(8,128)(2,1)S(1)}, bf16[256,384]{1,0:T(8,128)(2,1)S(1)}, u32[]{:S(2)}, u32[]{:S(2)}) collective-permute-start(bf16[256,384]{1,0:T(8,128)(2,1)S(1)} %convolution_convert_fusion.4), channel_id=1, source_target_pairs={{0,2},{2,4},{4,6},{6,8},{8,10},{10,12},{12,14},{14,16},{16,18},{18... | collective-permute-start | bytes 589832 | tf_op jit(solution)/shard_map/ppermute | solution.py:17
  147.4 52.2 %copy-start.46 = (f32[256,32]{0,1:T(8,128)}, f32[256,32]{0,1:T(8,128)S(1)}, u32[]{:S(2)}) copy-start(f32[256,32]{0,1:T(8,128)S(1)} %get-tuple-element.60) | copy-start | bytes 98308
  147.4 52.2 %copy-start.48 = (f32[256,32]{0,1:T(8,128)}, f32[256,32]{0,1:T(8,128)S(1)}, u32[]{:S(2)}) copy-start(f32[256,32]{0,1:T(8,128)S(1)} %get-tuple-element.61) | copy-start | bytes 98308
  147.5 105.1 %collective-permute-start.4 = (bf16[256,384]{0,1:T(8,128)(2,1)S(1)}, bf16[256,384]{0,1:T(8,128)(2,1)}, u32[]{:S(2)}, u32[]{:S(2)}) collective-permute-start(bf16[256,384]{0,1:T(8,128)(2,1)S(1)} %bitcast.201), channel_id=1, source_target_pairs={{0,8},{2,10},{4,12},{6,14},{8,16},{10,18},{12,20},{14,22},{16,24},... | collective-permute-start | bytes 589832 | tf_op jit(solution)/shard_map/ppermute | solution.py:17
  158.4 80.4 %copy-start.72 = (s32[256,2]{0,1:T(2,128)S(1)}, s32[256,2]{0,1:T(2,128)}, u32[]{:S(2)}) copy-start(s32[256,2]{0,1:T(2,128)} %param.32) | copy-start | bytes 6148
  199.6 57.1 %copy-start.40 = (f32[256,6,32]{0,2,1:T(8,128)}, f32[256,6,32]{0,2,1:T(8,128)S(1)}, u32[]{:S(2)}) copy-start(f32[256,6,32]{0,2,1:T(8,128)S(1)} %get-tuple-element.49) | copy-start | bytes 589828
  199.6 57.1 %copy-start.42 = (f32[256,6,32]{0,2,1:T(8,128)}, f32[256,6,32]{0,2,1:T(8,128)S(1)}, u32[]{:S(2)}) copy-start(f32[256,6,32]{0,2,1:T(8,128)S(1)} %get-tuple-element.50) | copy-start | bytes 589828
  239.5 14.3 collective-permute-start.5
  242.1 12.6 collective-permute-start.6
  244.8 10.9 collective-permute-start.7
  305.5 248.2 %copy-start.50 = (f32[256,16]{0,1:T(8,128)}, f32[256,16]{0,1:T(8,128)S(1)}, u32[]{:S(2)}) copy-start(f32[256,16]{0,1:T(8,128)S(1)} %get-tuple-element.30) | copy-start | bytes 49156
  311.7 36.3 %all-to-all-start = ((bf16[16,64,768]{2,1,0:T(8,128)(2,1)}), bf16[16,64,768]{2,1,0:T(8,128)(2,1)S(1)}, u32[]{:S(2)}, u32[]{:S(2)}) async-start(bf16[16,64,768]{2,1,0:T(8,128)(2,1)} %broadcast_select_fusion), calls=%async_computation | async-start | bytes 3145728 | tf_op jit(solution)/shard_map/all_to_all | solution.py:202
  315.6 143.5 %all-gather.5.cloned.1.call-start = ((), (), s32[]{:S(2)}) async-start(), calls=%async_computation.13 | async-start | bytes 1671168 | tf_op jit(solution)/shard_map/all_gather | solution.py:110
  348.1 30.7 %all-to-all-start.2 = ((bf16[16,64,768]{2,1,0:T(8,128)(2,1)}), bf16[16,64,768]{2,1,0:T(8,128)(2,1)}, u32[]{:S(2)}, u32[]{:S(2)}) async-start(bf16[16,64,768]{2,1,0:T(8,128)(2,1)} %select_convert_fusion), calls=%async_computation.2 | async-start | bytes 3145728 | tf_op jit(solution)/shard_map/all_to_all | solution.py:239
  357.7 113.9 %all-gather.7.cloned.1.call-start = ((), (), s32[]{:S(2)}) async-start(), calls=%async_computation.14 | async-start | bytes 1671168 | tf_op jit(solution)/shard_map/all_gather | solution.py:111
  393.2 58.7 %all-to-all-start.1 = ((bf16[16,64,768]{2,1,0:T(8,128)(2,1)}), bf16[16,64,768]{2,1,0:T(8,128)(2,1)S(1)}, u32[]{:S(2)}, u32[]{:S(2)}) async-start(bf16[16,64,768]{2,1,0:T(8,128)(2,1)} %convolution_convert_fusion), calls=%async_computation.1 | async-start | bytes 3145728 | tf_op jit(solution)/shard_map/all_to_all | solution.py:215
  419.8 111.9 %all-gather.9.cloned.1.call-start = ((), (), s32[]{:S(2)}) async-start(), calls=%async_computation.15 | async-start | bytes 1671168 | tf_op jit(solution)/shard_map/all_gather | solution.py:112
  451.9 102.4 %all-to-all-start.3 = ((bf16[16,64,768]{2,1,0:T(8,128)(2,1)}), bf16[16,64,768]{2,1,0:T(8,128)(2,1)}, u32[]{:S(2)}, u32[]{:S(2)}) async-start(bf16[16,64,768]{2,1,0:T(8,128)(2,1)} %add_convert_fusion), calls=%async_computation.3 | async-start | bytes 3145728 | tf_op jit(solution)/shard_map/all_to_all | solution.py:260
  458.2 125.8 %all-reduce.13.cloned.1.call-start = ((), (), s32[]{:S(2)}) async-start(), calls=%async_computation.16 | async-start | bytes 786432 | tf_op jit(solution)/shard_map/psum | solution.py:264
  474.5 61.9 %copy-start.9 = (bf16[768,1024]{1,0:T(8,128)(2,1)S(1)}, bf16[768,1024]{1,0:T(8,128)(2,1)}, u32[]{:S(2)}) copy-start(bf16[768,1024]{1,0:T(8,128)(2,1)} %all-gather.5.cloned.1.call-done) | copy-start | bytes 4718596
  566.9 128.3 %reduce-scatter.25.cloned.1.call-start = ((), (), s32[]{:S(2)}) async-start(), calls=%async_computation.24 | async-start | bytes 417792
  568.1 128.4 %all-reduce.15.cloned.1.call-start = ((), (), s32[]{:S(2)}) async-start(), calls=%async_computation.25 | async-start | bytes 1572864 | tf_op jit(solution)/shard_map/psum | solution.py:224
  603.2 10.0 collective-permute-start.11
  604.6 10.4 collective-permute-start.10
  605.9 13.0 collective-permute-start.9
  607.2 13.4 collective-permute-start.8
  608.7 22.8 %collective-permute-start.15 = (bf16[256,384]{0,1:T(8,128)(2,1)S(1)}, bf16[256,384]{0,1:T(8,128)(2,1)S(1)}, u32[]{:S(2)}, u32[]{:S(2)}) collective-permute-start(bf16[256,384]{0,1:T(8,128)(2,1)S(1)} %bitcast.196), channel_id=1, source_target_pairs={{8,0},{10,2},{12,4},{14,6},{16,8},{18,10},{20,12},{22,14},{24,16},... | collective-permute-start | bytes 589832 | tf_op jit(solution)/shard_map/ppermute | solution.py:17
  613.1 18.3 %collective-permute-start.14 = (bf16[256,384]{0,1:T(8,128)(2,1)S(1)}, bf16[256,384]{0,1:T(8,128)(2,1)S(1)}, u32[]{:S(2)}, u32[]{:S(2)}) collective-permute-start(bf16[256,384]{0,1:T(8,128)(2,1)S(1)} %bitcast.195), channel_id=1, source_target_pairs={{6,0},{8,2},{10,4},{12,6},{14,8},{16,10},{18,12},{20,14},{22,16},{... | collective-permute-start | bytes 589832 | tf_op jit(solution)/shard_map/ppermute | solution.py:17
  615.0 16.5 %collective-permute-start.13 = (bf16[256,384]{0,1:T(8,128)(2,1)S(1)}, bf16[256,384]{0,1:T(8,128)(2,1)S(1)}, u32[]{:S(2)}, u32[]{:S(2)}) collective-permute-start(bf16[256,384]{0,1:T(8,128)(2,1)S(1)} %bitcast.194), channel_id=1, source_target_pairs={{4,0},{6,2},{8,4},{10,6},{12,8},{14,10},{16,12},{18,14},{20,16},{2... | collective-permute-start | bytes 589832 | tf_op jit(solution)/shard_map/ppermute | solution.py:17
  618.9 13.1 collective-permute-start.12
  634.1 196.8 %reduce-scatter.19.cloned.1.call-start = ((), (), s32[]{:S(2)}) async-start(), calls=%async_computation.21 | async-start | bytes 3342336 | tf_op jit(solution)/shard_map/reduce_scatter | solution.py:340
  636.4 330.4 %reduce-scatter.21.cloned.1.call-start = ((), (), s32[]{:S(2)}) async-start(), calls=%async_computation.22 | async-start | bytes 3342336 | tf_op jit(solution)/shard_map/reduce_scatter | solution.py:341
  639.7 462.3 %reduce-scatter.23.cloned.1.call-start = ((), (), s32[]{:S(2)}) async-start(), calls=%async_computation.23 | async-start | bytes 3342336 | tf_op jit(solution)/shard_map/reduce_scatter | solution.py:342
  643.1 586.9 %reduce-scatter.17.cloned.1.call-start = ((), (), s32[]{:S(2)}) async-start(), calls=%async_computation.20 | async-start | bytes 1253376 | tf_op jit(solution)/shard_map/reduce_scatter | solution.py:337
  645.4 712.6 %reduce-scatter.11.cloned.1.call-start = ((), (), s32[]{:S(2)}) async-start(), calls=%async_computation.17 | async-start | bytes 1253376 | tf_op jit(solution)/shard_map/reduce_scatter | solution.py:334
  647.1 839.3 %reduce-scatter.13.cloned.1.call-start = ((), (), s32[]{:S(2)}) async-start(), calls=%async_computation.18 | async-start | bytes 1253376 | tf_op jit(solution)/shard_map/reduce_scatter | solution.py:335
  649.0 965.5 %reduce-scatter.15.cloned.1.call-start = ((), (), s32[]{:S(2)}) async-start(), calls=%async_computation.19 | async-start | bytes 1253376 | tf_op jit(solution)/shard_map/reduce_scatter | solution.py:336
  696.5 918.0 %copy-start.1 = (s32[4096]{0:T(1024)S(1)}, s32[4096]{0:T(1024)}, u32[]{:S(2)}) copy-start(s32[4096]{0:T(1024)} %param.33) | copy-start | bytes 49156
  (69 other events, 694.5 us)
Sparse Core Ops, SparseCore 0:
  265.5 16.9 all-reduce.10
  567.0 17.0 all-reduce.12
  634.2 30.7 all-reduce.14
Sparse Core Ops, SparseCore 1:
  319.8 79.3 all-gather.4
  402.8 68.7 all-gather.6
  475.1 56.5 all-gather.8
  573.0 122.1 reduce-scatter.24
  700.7 130.1 reduce-scatter.18
  836.5 130.2 reduce-scatter.20
  972.2 129.7 reduce-scatter.22
  1107.1 122.8 reduce-scatter.16
  1235.2 122.8 reduce-scatter.10
  1363.4 122.9 reduce-scatter.12
  1491.6 122.9 reduce-scatter.14
where the time goes:
time: 1630 us; the launch traced here: 1620 us
  waiting for transfers between devices  1050 us (64%)
  blocking collectives  282 us (17%)
  matrix products  99.8 us (6%)
  starting transfers between devices  76.4 us (5%)
  local copies, waits for them, and re-layouts  63.3 us (4%)
  other arithmetic  37.1 us (2%)
  between operations  18.9 us (1%)
    reduce_scatter x1, waiting for transfers between devices, local(): lax.psum_scatter(grad_sup, 'dp', scatter_dimension=0, tiled=True)  136 us
    reduce_scatter x1, waiting for transfers between devices, local(): lax.psum_scatter(grad_sdown, 'dp', scatter_dimension=1, tiled=True)  135 us
    reduce_scatter x1, waiting for transfers between devices, local(): lax.psum_scatter(grad_key, 'dp', scatter_dimension=0, tiled=True)  128 us
    reduce_scatter x1, waiting for transfers between devices, local(): lax.psum_scatter(grad_value, 'dp', scatter_dimension=0, tiled=True)  128 us
    reduce_scatter x1, waiting for transfers between devices, local(): lax.psum_scatter(grad_out, 'dp', scatter_dimension=1, tiled=True)  128 us
    reduce_scatter x1, waiting for transfers between devices, local(): lax.psum_scatter(grad_query, 'dp', scatter_dimension=0, tiled=True)  128 us
    reduce_scatter x1, waiting for transfers between devices, local(): lax.psum_scatter(grad_sgate, 'dp', scatter_dimension=0, tiled=True)  88.5 us
    unnamed x2, blocking collectives  77.5 us
  transfers between devices with their start and end apart: 34, of which 20 were waited for; matrix products, arithmetic and copies ran while one was open for 10% of the time, Pallas kernels for 0%

commit v1 on v0

v1 whole, which is shorter than its diff:
```python
import functools

import jax
import jax.numpy as jnp
from jax import lax
from jax.experimental import pallas as pl
from jax.experimental.pallas import tpu as pltpu
from jax.sharding import PartitionSpec as P

HEAD = 64
WINDOW = 1024
LANES = 128
PLANE = 4

MESH = pl.DeviceIdType.MESH
f32 = jnp.float32
bf16 = jnp.bfloat16

eps = 1e-06
masked = -1e30


def matmul(left, right):
    return jnp.dot(left, right, preferred_element_type=f32)


def weight_grad(left, right):
    return lax.dot_general(
        left, right, (((0,), (0,)), ((), ())), preferred_element_type=f32
    )


def input_grad(left, right):
    return lax.dot_general(
        left, right, (((1,), (1,)), ((), ())), preferred_element_type=f32
    )


def rms_parts(values):
    factor = lax.rsqrt(jnp.mean(values * values, axis=-1, keepdims=True) + eps)
    return (values * factor, factor)


def rotary_tables(positions):
    freqs = 10000.0 ** (-jnp.arange(HEAD // 2, dtype=f32) * (2.0 / HEAD))
    phase = positions.astype(f32)[:, None] * freqs[None, :]
    return (jnp.cos(phase)[:, None, :], jnp.sin(phase)[:, None, :])


def rotate(values, cosines, sines):
    half = values.shape[-1] // 2
    first = values[..., :half]
    second = values[..., half:]
    return jnp.concatenate(
        [first * cosines - second * sines, second * cosines + first * sines], axis=-1
    )


def unrotate(grads, cosines, sines):
    half = grads.shape[-1] // 2
    first = grads[..., :half]
    second = grads[..., half:]
    return jnp.concatenate(
        [first * cosines + second * sines, second * cosines - first * sines], axis=-1
    )


def silu_grad(values):
    sigma = jax.nn.sigmoid(values)
    return sigma * (1.0 + values * (1.0 - sigma))


def masked_scores(queries, keys, valid):
    scores = jnp.einsum("qhe,khe->hqk", queries, keys, preferred_element_type=f32)
    return jnp.where(valid[None, :, :], scores, masked)


def digits(me):
    return lax.div(me, PLANE), lax.rem(lax.div(me, 2), 2), lax.rem(me, 2)


def index_of(z, y, x):
    return z * PLANE + y * 2 + x


def push(src, dst, send, recv, device):
    copy = pltpu.make_async_remote_copy(
        src_ref=src,
        dst_ref=dst,
        send_sem=send,
        recv_sem=recv,
        device_id=device,
        device_id_type=MESH,
    )
    copy.start()
    return copy


def greet(devices):
    barrier = pltpu.get_barrier_semaphore()
    for device in devices:
        pl.semaphore_signal(barrier, inc=1, device_id=device, device_id_type=MESH)
    pl.semaphore_wait(barrier, len(devices))


def comm_params(collective_id, limit=48 << 20):
    return pltpu.CompilerParams(
        collective_id=collective_id, has_side_effects=True, vmem_limit_bytes=limit
    )


def dma(*shape):
    return pltpu.SemaphoreType.DMA(shape)


IN_HBM = pl.BlockSpec(memory_space=pl.ANY)
IN_VMEM = pl.BlockSpec(memory_space=pltpu.VMEM)


def grid_peers(depth, z, y, x):
    peers = [{"dp": index_of(lax.rem(z + k, depth), y, x)} for k in range(1, depth)]
    return peers, {"dp": index_of(z, 1 - y, x)}, {"dp": index_of(z, y, 1 - x)}


def gather_kernel(
    depth, reach, cuts, shard, tok, full, window,
    z_send, z_recv, p_send, p_recv, t_send, t_recv, f_send, f_recv, own,
):
    n = depth * PLANE
    me, core = lax.axis_index("dp"), lax.axis_index("tensor")
    z, y, x = digits(me)
    z_peers, y_peer, x_peer = grid_peers(depth, z, y, x)
    sibling = {"tensor": 1 - core}
    ahead = [{"dp": lax.rem(me + k, n)} for k in range(1, reach + 1)]
    behind = [{"dp": lax.rem(me + n - k, n)} for k in range(1, reach + 1)]
    greet(z_peers + [y_peer, x_peer, sibling] + ahead + behind)
    own_shard = pltpu.make_async_copy(shard, full.at[z, y, x], own.at[0])
    own_shard.start()
    own_tok = pltpu.make_async_copy(tok, window.at[reach], own.at[1])
    own_tok.start()
    half = tok.shape[0] // 2
    rows = pl.ds(pl.multiple_of(core * half, half), half)
    z_copies = []
    t_copies = []
    for c, (start, middle, stop) in enumerate(cuts):
        cols = pl.ds(start, stop - start)
        z_copies.append(
            [
                push(
                    shard.at[:, cols],
                    full.at[z, y, x, :, cols],
                    z_send.at[c, k],
                    z_recv.at[c, k],
                    z_peers[k],
                )
                for k in range(depth - 1)
            ]
        )
        if c == 0:
            for k in range(reach):
                t_copies.append(
                    push(
                        tok.at[rows],
                        window.at[reach - 1 - k, rows],
                        t_send.at[k],
                        t_recv.at[k],
                        ahead[k],
                    )
                )
    own_shard.wait()
    second, third, forwards = [], [], []
    for c in range(len(cuts) + 2):
        if c < len(cuts):
            start, middle, stop = cuts[c]
            left, right = pl.ds(start, middle - start), pl.ds(middle, stop - middle)
            for copy in z_copies[c]:
                copy.wait_recv()
            second.append(
                [
                    push(
                        full.at[:, y, x, :, left],
                        full.at[:, y, x, :, left],
                        p_send.at[c, 0],
                        p_recv.at[c, 0],
                        y_peer,
                    ),
                    push(
                        full.at[:, y, x, :, right],
                        full.at[:, y, x, :, right],
                        p_send.at[c, 1],
                        p_recv.at[c, 1],
                        x_peer,
                    ),
                ]
            )
        if c == 0:
            for k, copy in enumerate(t_copies):
                copy.wait_recv()
                forwards.append(
                    push(
                        window.at[reach - 1 - k, rows],
                        window.at[reach - 1 - k, rows],
                        f_send.at[k],
                        f_recv.at[k],
                        sibling,
                    )
                )
        if 1 <= c <= len(cuts):
            start, middle, stop = cuts[c - 1]
            left, right = pl.ds(start, middle - start), pl.ds(middle, stop - middle)
            for copy in second[c - 1]:
                copy.wait_recv()
            third.append(
                [
                    push(
                        full.at[:, :, x, :, left],
                        full.at[:, :, x, :, left],
                        p_send.at[c - 1, 2],
                        p_recv.at[c - 1, 2],
                        x_peer,
                    ),
                    push(
                        full.at[:, y, :, :, right],
                        full.at[:, y, :, :, right],
                        p_send.at[c - 1, 3],
                        p_recv.at[c - 1, 3],
                        y_peer,
                    ),
                ]
            )
    for copies in third:
        for copy in copies:
            copy.wait_recv()
    for copy in forwards:
        copy.wait_recv()
    own_tok.wait()
    for copies in z_copies + second + third + [t_copies, forwards]:
        for copy in copies:
            copy.wait_send()


def gather_all(shard, tokens, depth, reach, cuts):
    parts = len(cuts)
    full, window = pl.pallas_call(
        functools.partial(gather_kernel, depth, reach, cuts),
        out_shape=(
            jax.ShapeDtypeStruct((depth, 2, 2) + shard.shape, shard.dtype),
            jax.ShapeDtypeStruct((reach + 1,) + tokens.shape, tokens.dtype),
        ),
        in_specs=[IN_HBM] * 2,
        out_specs=(IN_HBM, IN_HBM),
        scratch_shapes=[
            dma(parts, depth - 1), dma(parts, depth - 1), dma(parts, 4), dma(parts, 4),
            dma(reach), dma(reach), dma(reach), dma(reach), dma(2),
        ],
        compiler_params=comm_params(1),
        name="gather_weights",
    )(shard, tokens)
    return full.reshape(-1, shard.shape[1]), window.reshape(-1, tokens.shape[1])


def swap_kernel(count, *refs):
    sources, targets, (send, recv) = refs[:count], refs[count : 2 * count], refs[2 * count :]
    sibling = {"tensor": 1 - lax.axis_index("tensor")}
    greet([sibling])
    copies = [
        push(a, b, send.at[i], recv.at[i], sibling)
        for i, (a, b) in enumerate(zip(sources, targets))
    ]
    for copy in copies:
        copy.wait()


def swap(arrays, collective_id):
    count = len(arrays)
    return pl.pallas_call(
        functools.partial(swap_kernel, count),
        out_shape=tuple(jax.ShapeDtypeStruct(a.shape, a.dtype) for a in arrays),
        in_specs=[IN_VMEM] * count,
        out_specs=(IN_VMEM,) * count,
        scratch_shapes=[dma(count), dma(count)],
        compiler_params=comm_params(collective_id),
        name="swap_cores",
    )(*arrays)


def dispatch_kernel(n, owners, first, second, got_first, got_second, send, recv, f_send, f_recv, own):
    me, core = lax.axis_index("dp"), lax.axis_index("tensor")
    sibling = {"tensor": 1 - core}
    greet([{"dp": lax.rem(me + k, n)} for k in range(1, n)] + [sibling])
    half = first.shape[-1] // 2
    cols = pl.ds(pl.multiple_of(core * half, half), half)
    pairs = ((first, got_first), (second, got_second))
    mine = lax.div(me, owners)
    copies = []
    for k in range(1, n):
        to = lax.rem(me + k, n)
        for i, (source, target) in enumerate(pairs):
            copies.append(
                push(
                    source.at[lax.div(to, owners), :, cols],
                    target.at[me, :, cols],
                    send.at[i, k],
                    recv.at[i, k],
                    {"dp": to},
                )
            )
    local = [
        pltpu.make_async_copy(source.at[mine], target.at[me], own.at[i])
        for i, (source, target) in enumerate(pairs)
    ]
    for copy in local:
        copy.start()
    forwards = []
    for k in range(1, n):
        source_of = lax.rem(me + n - k, n)
        for i, (source, target) in enumerate(pairs):
            copies[2 * (k - 1) + i].wait_recv()
            block = target.at[source_of, :, cols]
            forwards.append(push(block, block, f_send.at[i, k], f_recv.at[i, k], sibling))
    for copy in forwards:
        copy.wait_recv()
    for copy in local:
        copy.wait()
    for copy in copies + forwards:
        copy.wait_send()


def dispatch(first, second, n, owners):
    shape = jax.ShapeDtypeStruct((n,) + first.shape[1:], first.dtype)
    return pl.pallas_call(
        functools.partial(dispatch_kernel, n, owners),
        out_shape=(shape, shape),
        in_specs=[IN_HBM] * 2,
        out_specs=(IN_HBM, IN_HBM),
        scratch_shapes=[dma(2, n), dma(2, n), dma(2, n), dma(2, n), dma(2)],
        compiler_params=comm_params(2),
        name="dispatch_rows",
    )(first, second)


def return_kernel(n, groups, first, second, got_first, got_second, part, total, send, recv, f_send, f_recv, own):
    me, core = lax.axis_index("dp"), lax.axis_index("tensor")
    sibling = {"tensor": 1 - core}
    greet([{"dp": lax.rem(me + k, n)} for k in range(1, n)] + [sibling])
    half = first.shape[-1] // 2
    mine = pl.ds(pl.multiple_of(core * half, half), half)
    theirs = pl.ds(pl.multiple_of((1 - core) * half, half), half)
    pairs = ((first, got_first), (second, got_second))
    each = n // groups
    swaps = []
    for g in range(groups):
        block = pl.ds(g * each, each)
        for i, (source, target) in enumerate(pairs):
            swaps.append(
                push(
                    source.at[block, :, theirs],
                    part.at[i, block],
                    f_send.at[i, g],
                    f_recv.at[i, g],
                    sibling,
                )
            )
    for g in range(groups):
        block = pl.ds(g * each, each)
        for i, (source, target) in enumerate(pairs):
            swaps[2 * g + i].wait_recv()
            total[i, block] = (
                source[block, :, mine].astype(f32) + part[i, block].astype(f32)
            ).astype(bf16)
        for slot in range(g * each, (g + 1) * each):
            for i, (source, target) in enumerate(pairs):
                @pl.when(slot != me)
                def _():
                    push(
                        total.at[i, slot],
                        target.at[me],
                        send.at[i, slot],
                        recv.at[i, me],
                        {"dp": slot},
                    )
    local = [
        pltpu.make_async_copy(total.at[i, me], pairs[i][1].at[me], own.at[i]) for i in range(2)
    ]
    for copy in local:
        copy.start()
    for k in range(1, n):
        to, source_of = lax.rem(me + k, n), lax.rem(me + n - k, n)
        for i, (source, target) in enumerate(pairs):
            pltpu.make_async_remote_copy(
                total.at[i, to], target.at[source_of], send.at[i, to], recv.at[i, source_of],
                device_id={"dp": to}, device_id_type=MESH,
            ).wait()
    for copy in local:
        copy.wait()
    for copy in swaps:
        copy.wait_send()


def give_back(first, second, groups=4):
    n, capacity, width = first.shape
    half = jax.ShapeDtypeStruct((n, capacity, width // 2), first.dtype)
    buffer = pltpu.VMEM((2, n, capacity, width // 2), first.dtype)
    return pl.pallas_call(
        functools.partial(return_kernel, n, groups),
        out_shape=(half, half),
        in_specs=[IN_VMEM] * 2,
        out_specs=(IN_HBM, IN_HBM),
        scratch_shapes=[buffer, buffer, dma(2, n), dma(2, n), dma(2, groups), dma(2, groups), dma(2)],
        compiler_params=comm_params(3),
        name="return_rows",
    )(first, second)


def scatter_kernel(
    depth, reach, cuts, per_core, grads, d_part, total, d_full,
    first_l, first_r, second_l, second_r, last, d_swap, d_sum, d_got, gain_got,
    p_send, p_recv, z_send, z_recv, t_send, t_recv, f_send, f_recv,
):
    n = depth * PLANE
    me, core = lax.axis_index("dp"), lax.axis_index("tensor")
    z, y, x = digits(me)
    z_peers, y_peer, x_peer = grid_peers(depth, z, y, x)
    sibling = {"tensor": 1 - core}
    ahead = [{"dp": lax.rem(me + k, n)} for k in range(1, reach + 1)]
    behind = [{"dp": lax.rem(me + n - k, n)} for k in range(1, reach + 1)]
    greet(z_peers + [y_peer, x_peer, sibling] + ahead + behind)
    width = d_part.shape[-1] // 2
    mine = pl.ds(pl.multiple_of(core * width, width), width)
    theirs = pl.ds(pl.multiple_of((1 - core) * width, width), width)
    swapped = push(d_part.at[:, :, theirs], d_swap, f_send.at[0], f_recv.at[0], sibling)
    ones = []
    for c, (start, middle, stop) in enumerate(cuts):
        left, right = pl.ds(start, middle - start), pl.ds(middle, stop - middle)
        ones.append(
            [
                push(
                    grads.at[:, :, 1 - x, :, left],
                    first_l.at[:, :, :, pl.ds(start // 2, middle - start)],
                    p_send.at[c, 0], p_recv.at[c, 0], x_peer,
                ),
                push(
                    grads.at[:, 1 - y, :, :, right],
                    first_r.at[:, :, :, pl.ds(start // 2, stop - middle)],
                    p_send.at[c, 1], p_recv.at[c, 1], y_peer,
                ),
            ]
        )
    swapped.wait_recv()
    d_sum[...] = (d_part[:, :, mine].astype(f32) + d_swap[...].astype(f32)).astype(bf16)
    back = [
        push(d_sum.at[reach - 1 - k], d_got.at[k], t_send.at[k], t_recv.at[k], behind[k])
        for k in range(reach)
    ]
    twos, threes = [], []
    for c in range(len(cuts) + 2):
        if c < len(cuts):
            start, middle, stop = cuts[c]
            span = middle - start
            left, right = pl.ds(start, span), pl.ds(middle, span)
            here = pl.ds(start // 2, span)
            for copy in ones[c]:
                copy.wait_recv()

            def add_first(i, carry):
                for j in range(2):
                    first_l[i, j, :, here] = (
                        first_l[i, j, :, here].astype(f32) + grads[i, j, x, :, left].astype(f32)
                    ).astype(bf16)
                    first_r[i, j, :, here] = (
                        first_r[i, j, :, here].astype(f32) + grads[i, y, j, :, right].astype(f32)
                    ).astype(bf16)
                return carry

            lax.fori_loop(0, depth, add_first, 0)
            twos.append(
                [
                    push(
                        first_l.at[:, 1 - y, :, here], second_l.at[:, :, here],
                        p_send.at[c, 2], p_recv.at[c, 2], y_peer,
                    ),
                    push(
                        first_r.at[:, 1 - x, :, here], second_r.at[:, :, here],
                        p_send.at[c, 3], p_recv.at[c, 3], x_peer,
                    ),
                ]
            )
        if 1 <= c <= len(cuts):
            start, middle, stop = cuts[c - 1]
            span = middle - start
            here = pl.ds(start // 2, span)
            for copy in twos[c - 1]:
                copy.wait_recv()

            def add_second(i, carry):
                second_l[i, :, here] = (
                    second_l[i, :, here].astype(f32) + first_l[i, y, :, here].astype(f32)
                ).astype(bf16)
                second_r[i, :, here] = (
                    second_r[i, :, here].astype(f32) + first_r[i, x, :, here].astype(f32)
                ).astype(bf16)
                return carry

            lax.fori_loop(0, depth, add_second, 0)
            threes.append(
                [
                    push(
                        source.at[lax.rem(z + k + 1, depth), :, here],
                        last.at[k, side, :, here],
                        z_send.at[c - 1, side, k], z_recv.at[c - 1, side, k], z_peers[k],
                    )
                    for side, source in ((0, second_l), (1, second_r))
                    for k in range(depth - 1)
                ]
            )
        if c >= 2:
            start, middle, stop = cuts[c - 2]
            span = middle - start
            here = pl.ds(start // 2, span)
            for copy in threes[c - 2]:
                copy.wait_recv()
            for side, source, at in ((0, second_l, start), (1, second_r, middle)):
                value = source[z, :, here].astype(f32)
                for k in range(depth - 1):
                    value = value + last[k, side, :, here].astype(f32)
                total[:, pl.ds(at, span)] = value
    d_mine = d_sum[reach].astype(f32)
    for k, copy in enumerate(back):
        copy.wait_recv()
        d_mine = d_mine + d_got[k].astype(f32)
    d_full[:, mine] = d_mine.astype(bf16)
    both = push(d_full.at[:, mine], d_full.at[:, mine], f_send.at[1], f_recv.at[1], sibling)
    split = pl.ds(per_core, LANES)
    gain = push(total.at[:, split], gain_got, f_send.at[2], f_recv.at[2], sibling)
    both.wait_recv()
    gain.wait()
    total[:, split] = total[:, split] + gain_got[...]
    for copies in ones + twos + threes + [back, [swapped, both]]:
        for copy in copies:
            copy.wait_send()


def scatter_all(grads, d_part, per_core, depth, reach, cuts):
    rows, columns = grads.shape[0] // (depth * PLANE), grads.shape[1]
    grads = grads.reshape(depth, 2, 2, rows, columns)
    count, width = d_part.shape[0] // (reach + 1), d_part.shape[1]
    d_part = d_part.reshape(reach + 1, count, width)
    parts, half = len(cuts), columns // 2
    first = pltpu.VMEM((depth, 2, rows, half), bf16)
    second = pltpu.VMEM((depth, rows, half), bf16)
    return pl.pallas_call(
        functools.partial(scatter_kernel, depth, reach, cuts, per_core),
        out_shape=(
            jax.ShapeDtypeStruct((rows, columns), f32),
            jax.ShapeDtypeStruct((count, width), bf16),
        ),
        in_specs=[IN_VMEM] * 2,
        out_specs=(IN_VMEM, IN_VMEM),
        scratch_shapes=[
            first, first, second, second,
            pltpu.VMEM((depth - 1, 2, rows, half), bf16),
            pltpu.VMEM((reach + 1, count, width // 2), bf16),
            pltpu.VMEM((reach + 1, count, width // 2), bf16),
            pltpu.VMEM((reach, count, width // 2), bf16),
            pltpu.VMEM((rows, LANES), f32),
            dma(parts, 4), dma(parts, 4),
            dma(parts, 2, depth - 1), dma(parts, 2, depth - 1),
            dma(reach), dma(reach), dma(3), dma(3),
        ],
        compiler_params=comm_params(4),
        name="scatter_grads",
    )(grads, d_part)


def local(
    tokens, cotangent, attn_gain, w_query, w_key, w_value, w_out, ffn_gain, w_router,
    w_sgate, w_sup, w_sdown, e_gate, e_up, e_down, routes, segments,
):
    tok_count, width = tokens.shape
    n = lax.axis_size("dp")
    depth = n // PLANE
    me = lax.axis_index("dp")
    core = lax.axis_index("tensor")
    experts = w_router.shape[1]
    owners = n // experts
    capacity = tok_count // 4
    reach = (WINDOW + tok_count - 1) // tok_count
    score_scale = HEAD ** (-0.5)
    shard_rows = w_query.shape[0]
    heads_width = w_query.shape[1]
    local_heads = heads_width // HEAD
    hidden = w_sgate.shape[1]
    half = width // 2

    small = 2 * LANES
    packed = jnp.concatenate(
        [
            w_query, w_key, w_value, w_out.T,
            jnp.pad(
                jnp.concatenate([w_router, attn_gain[:, None], ffn_gain[:, None]], axis=1),
                ((0, 0), (0, small - experts - 2)),
            ),
            w_sgate, w_sup, w_sdown.T,
        ],
        axis=1,
    ).astype(bf16)
    at_small = 4 * heads_width
    at_shared = at_small + small
    columns = at_shared + 3 * hidden
    edges = [0, at_small, at_shared + hidden, at_shared + 2 * hidden, columns]
    cuts = tuple((a, (a + b) // 2, b) for a, b in zip(edges[:-1], edges[1:]))
    full, window = gather_all(packed, tokens, depth, reach, cuts)
    query_w = full[:, :heads_width]
    key_w = full[:, heads_width : 2 * heads_width]
    value_w = full[:, 2 * heads_width : 3 * heads_width]
    out_t = full[:, 3 * heads_width : at_small]
    router_w = full[:, at_small : at_small + experts]
    gain_first = full[:, at_small + experts].astype(f32)
    gain_second = full[:, at_small + experts + 1].astype(f32)
    sgate_w = full[:, at_shared : at_shared + hidden]
    sup_w = full[:, at_shared + hidden : at_shared + 2 * hidden]
    sdown_t = full[:, at_shared + 2 * hidden :]
    expert_gate = e_gate.astype(bf16)
    expert_up = e_up.astype(bf16)
    expert_down = e_down.astype(bf16)

    span = (reach + 1) * tok_count
    token_rows = me * tok_count + jnp.arange(tok_count, dtype=jnp.int32)
    key_rows = (me - reach) * tok_count + jnp.arange(span, dtype=jnp.int32)
    cos_all, sin_all = rotary_tables(key_rows)
    cosines, sines = cos_all[reach * tok_count :], sin_all[reach * tok_count :]
    padded = jnp.pad(segments, (reach * tok_count, 0), constant_values=-1)
    seg_key = lax.dynamic_slice_in_dim(padded, me * tok_count, span)
    seg_query = seg_key[reach * tok_count :]
    later, earlier = token_rows[:, None], key_rows[None, :]
    valid = (earlier >= 0) & (earlier <= later) & (later - earlier < WINDOW)
    valid = valid & (seg_key[None, :] == seg_query[:, None])
    head_shape = (tok_count, local_heads, HEAD)
    span_shape = (span, local_heads, HEAD)
    x_all = window.astype(f32)
    normed_all, scale_all = rms_parts(x_all)
    attn_in_all = (normed_all * gain_first).astype(bf16)
    attn_in = attn_in_all[reach * tok_count :]
    x_float = tokens.astype(f32)
    normed_one, scale_one = rms_parts(x_float)
    queries = (
        rotate(matmul(attn_in, query_w).reshape(head_shape), cosines, sines) * score_scale
    ).astype(bf16)
    all_keys = rotate(matmul(attn_in_all, key_w).reshape(span_shape), cos_all, sin_all).astype(bf16)
    all_values = matmul(attn_in_all, value_w).astype(bf16).reshape(span_shape)
    scores = masked_scores(queries, all_keys, valid)
    peak = jnp.max(scores, axis=-1, keepdims=True)
    lse = peak + jnp.log(jnp.sum(jnp.exp(scores - peak), axis=-1, keepdims=True))
    weights = jnp.exp(scores - lse)
    heads_out = (
        jnp.einsum("hqk,khe->qhe", weights.astype(bf16), all_values, preferred_element_type=f32)
        .astype(bf16)
        .reshape(tok_count, -1)
    )
    out_part = input_grad(heads_out, out_t).astype(bf16)
    (out_other,) = swap([out_part], 5)
    middle = x_float + (out_part.astype(f32) + out_other.astype(f32))

    normed_two, scale_two = rms_parts(middle)
    branch_in = (normed_two * gain_second).astype(bf16)
    logits = matmul(branch_in, router_w)
    expo = jnp.exp(logits - jnp.max(logits, axis=-1, keepdims=True))
    probs = expo / jnp.sum(expo, axis=-1, keepdims=True)
    picked = (routes[:, :, None] == jnp.arange(experts, dtype=jnp.int32)[None, None, :]).astype(f32)
    gates = jnp.sum(probs[:, None, :] * picked, axis=2)
    chosen = jnp.sum(picked, axis=1)
    places = jnp.arange(tok_count, dtype=jnp.int32)
    below = (places[:, None] > places[None, :]).astype(bf16)
    before = matmul(below, chosen.astype(bf16))
    slots = jnp.arange(capacity, dtype=f32)
    taken = (before.T[:, None, :] == slots[None, :, None]) & (chosen.T[:, None, :] > 0.5)
    gate_slot = jnp.sum(jnp.where(taken, probs.T[:, None, :], 0.0), axis=2)
    chooser = taken.astype(bf16).reshape(experts * capacity, tok_count)
    pair_slot = routes * capacity + jnp.sum(picked * before[:, None, :], axis=2).astype(jnp.int32)
    all_slots = jnp.arange(experts * capacity, dtype=jnp.int32)
    pick = [(pair_slot[:, k : k + 1] == all_slots[None, :]).astype(bf16) for k in range(routes.shape[1])]
    rows_out = matmul(chooser, branch_in).astype(bf16).reshape(experts, capacity, width)
    d_after = cotangent.astype(f32)
    d_rows_out = (
        gate_slot.reshape(-1, 1) * matmul(chooser, cotangent)
    ).astype(bf16).reshape(experts, capacity, width)
    rows_in, d_rows_in = dispatch(rows_out, d_rows_out, n, owners)

    rows_in = rows_in.reshape(n * capacity, width)
    d_rows_in = d_rows_in.reshape(n * capacity, width)
    gate_hidden = matmul(rows_in, expert_gate)
    up_hidden = matmul(rows_in, expert_up)
    gate_act = jax.nn.silu(gate_hidden)
    expert_hidden = (gate_act * up_hidden).astype(bf16)
    part_rows = matmul(expert_hidden, expert_down).astype(bf16)
    d_hidden = input_grad(d_rows_in, expert_down)
    d_gate_hidden = (d_hidden * up_hidden * silu_grad(gate_hidden)).astype(bf16)
    d_up_hidden = (d_hidden * gate_act).astype(bf16)
    d_part_rows = (
        input_grad(d_gate_hidden, expert_gate) + input_grad(d_up_hidden, expert_up)
    ).astype(bf16)
    returned, d_returned = give_back(
        part_rows.reshape(n, capacity, width), d_part_rows.reshape(n, capacity, width)
    )
    grad_e_down = weight_grad(expert_hidden, d_rows_in)
    grad_e_gate = weight_grad(rows_in, d_gate_hidden)
    grad_e_up = weight_grad(rows_in, d_up_hidden)

    shared_gate = matmul(branch_in, sgate_w)
    shared_up = matmul(branch_in, sup_w)
    shared_act = jax.nn.silu(shared_gate)
    shared_hidden = (shared_act * shared_up).astype(bf16)
    shared_part = input_grad(shared_hidden, sdown_t)
    d_shared = matmul(cotangent, sdown_t)
    grad_sdown_t = weight_grad(cotangent, shared_hidden)
    d_sgate = (d_shared * shared_up * silu_grad(shared_gate)).astype(bf16)
    d_sup = (d_shared * shared_act).astype(bf16)
    grad_sgate = weight_grad(branch_in, d_sgate)
    grad_sup = weight_grad(branch_in, d_sup)
    d_shared_in = input_grad(d_sgate, sgate_w) + input_grad(d_sup, sup_w)

    def incoming(rows):
        rows = rows.reshape(experts, owners, capacity, half)
        if owners > 1:
            rows = jnp.sum(rows.astype(f32), axis=1).astype(bf16)
        return rows.reshape(experts * capacity, half)

    def placed(values):
        own = jnp.concatenate([values, jnp.zeros_like(values)], axis=1)
        other = jnp.concatenate([jnp.zeros_like(values), values], axis=1)
        return jnp.where(core == 0, own, other)

    result_rows, d_result_rows = incoming(returned), incoming(d_returned)
    pair_out = [matmul(p, result_rows) for p in pick]
    d_pairs = matmul(sum(pick), d_result_rows)
    moe_half = sum(gates[:, k : k + 1] * pair_out[k] for k in range(len(pick)))
    d_half = lax.dynamic_slice_in_dim(cotangent, core * half, half, axis=1).astype(f32)
    d_gates_part = jnp.concatenate(
        [jnp.sum(d_half * p, axis=1, keepdims=True) for p in pair_out], axis=1
    )
    after_part = (placed(moe_half) + shared_part).astype(bf16)
    d_branch_part = (d_shared_in + placed(d_pairs)).astype(bf16)
    d_gates_part = jnp.pad(d_gates_part, ((0, 0), (0, LANES - len(pick))))
    after_other, d_branch_other, d_gates_other = swap(
        [after_part, d_branch_part, d_gates_part], 6
    )
    output = (middle + (after_part.astype(f32) + after_other.astype(f32))).astype(bf16)
    d_branch_sum = d_branch_part.astype(f32) + d_branch_other.astype(f32)
    d_gates = (d_gates_part + d_gates_other)[:, : len(pick)]
    d_probs = jnp.sum(d_gates[:, :, None] * picked, axis=1)
    d_logits = (probs * (d_probs - jnp.sum(probs * d_probs, axis=-1, keepdims=True))).astype(bf16)
    grad_router = weight_grad(branch_in, d_logits)
    d_branch_in = d_branch_sum + input_grad(d_logits, router_w)
    grad_gain_two = jnp.sum(d_branch_in * normed_two, axis=0)
    d_norm_two = d_branch_in * gain_second
    d_middle = d_after + scale_two * (
        d_norm_two - normed_two * jnp.mean(d_norm_two * normed_two, axis=-1, keepdims=True)
    )

    d_attn = d_middle.astype(bf16)
    grad_out_t = weight_grad(d_attn, heads_out)
    d_heads = matmul(d_attn, out_t).astype(bf16).reshape(head_shape)
    again = jnp.exp(masked_scores(queries, all_keys, valid) - lse)
    d_weights = jnp.einsum("qhe,khe->hqk", d_heads, all_values, preferred_element_type=f32)
    d_scores = (again * (d_weights - jnp.sum(again * d_weights, axis=-1, keepdims=True))).astype(bf16)
    d_queries = (
        jnp.einsum("hqk,khe->qhe", d_scores, all_keys, preferred_element_type=f32) * score_scale
    )
    d_keys = jnp.einsum("hqk,qhe->khe", d_scores, queries, preferred_element_type=f32)
    d_values = jnp.einsum("hqk,qhe->khe", again.astype(bf16), d_heads, preferred_element_type=f32)
    d_query_pre = unrotate(d_queries, cosines, sines).astype(bf16).reshape(tok_count, -1)
    d_key_pre = unrotate(d_keys, cos_all, sin_all).astype(bf16).reshape(span, -1)
    d_value_pre = d_values.astype(bf16).reshape(span, -1)
    grad_query = weight_grad(attn_in, d_query_pre)
    grad_key = weight_grad(attn_in_all, d_key_pre)
    grad_value = weight_grad(attn_in_all, d_value_pre)
    d_attn_part = input_grad(d_key_pre, key_w) + input_grad(d_value_pre, value_w)
    d_attn_part = jnp.concatenate(
        [
            d_attn_part[: reach * tok_count],
            d_attn_part[reach * tok_count :] + input_grad(d_query_pre, query_w),
        ],
        axis=0,
    )
    grad_gain_one = jnp.sum(d_attn_part * normed_all, axis=0)
    grad_small = jnp.concatenate(
        [
            grad_router,
            grad_gain_two[:, None],
            jnp.zeros((width, LANES - experts - 1), f32),
            grad_gain_one[:, None],
            jnp.zeros((width, small - LANES - 1), f32),
        ],
        axis=1,
    )
    grads = jnp.concatenate(
        [grad_query, grad_key, grad_value, grad_out_t, grad_small, grad_sgate, grad_sup, grad_sdown_t],
        axis=1,
    ).astype(bf16)
    total, d_attn_in = scatter_all(grads, d_attn_part.astype(bf16), at_small + LANES, depth, reach, cuts)
    d_attn_in = d_attn_in.astype(f32)
    d_norm_one = d_attn_in * gain_first
    token_input_gradient = d_middle + scale_one * (
        d_norm_one - normed_one * jnp.mean(d_norm_one * normed_one, axis=-1, keepdims=True)
    )
    return (
        output,
        token_input_gradient,
        total[:, at_small + LANES],
        total[:, :heads_width],
        total[:, heads_width : 2 * heads_width],
        total[:, 2 * heads_width : 3 * heads_width],
        total[:, 3 * heads_width : at_small].T,
        total[:, at_small + experts],
        total[:, at_small : at_small + experts],
        total[:, at_shared : at_shared + hidden],
        total[:, at_shared + hidden : at_shared + 2 * hidden],
        total[:, at_shared + 2 * hidden :].T,
        grad_e_gate,
        grad_e_up,
        grad_e_down,
    )


def solution(mesh):
    by_dp, both, turned = P("dp", None), P("dp", "tensor"), P("tensor", "dp")
    wide, tall = P(None, ("dp", "tensor")), P(("dp", "tensor"), None)
    weights = (P("dp"), both, both, both, turned, P("dp"), by_dp, both, both, turned, wide, wide, tall)
    return jax.shard_map(
        local,
        mesh=mesh,
        in_specs=(by_dp, by_dp) + weights + (by_dp, P()),
        out_specs=(by_dp, by_dp) + weights,
        check_vma=False,
    )
```

time: 1630 us -> 493 us (0.30)
  waiting for transfers between devices: 1050 us -> 0 us
  Pallas kernels: 0 us -> 308 us
  blocking collectives: 282 us -> 0 us
  starting transfers between devices: 76.4 us -> 0 us
  local copies, waits for them, and re-layouts: 63.3 us -> 43.8 us
  between operations: 18.9 us -> 2.52 us
    reduce_scatter x7 -> x0, waiting for transfers between devices: 872 us -> none  [the longest x1 136 us: local(): lax.psum_scatter(grad_sup, 'dp', scatter_dimension=0, tiled=True)]
    pallas_call x0 -> x6, Pallas kernels: none -> 308 us  [the longest x1 114 us: scatter_all(): pl.pallas_call(functools.partial(scatter_kernel, depth, reach, cuts, per_...]
    all_gather x5 -> x0, blocking collectives: 202 us -> none  [the longest x1 45.7 us: local(): lax.all_gather(w_value.astype(jnp.bfloat16), 'dp', axis=0, tiled=True)]
    unnamed x2 -> x0, blocking collectives: 77.5 us -> none
    all_gather x3 -> x0, waiting for transfers between devices: 66.7 us -> none  [the longest x1 57.2 us: local(): lax.all_gather(w_sdown.astype(jnp.bfloat16), 'dp', axis=1, tiled=True)]
    all_to_all x4 -> x0, waiting for transfers between devices: 48.4 us -> none  [the longest x1 23.9 us: local(): lax.all_to_all(partial_rows, 'dp', split_axis=0, concat_axis=0, tiled=True)]
    all_to_all x4 -> x0, starting transfers between devices: 46.3 us -> none  [the longest x1 26.6 us: local(): lax.all_to_all(partial_rows, 'dp', split_axis=0, concat_axis=0, tiled=True)]
    gather x11 -> x0, local copies, waits for them, and re-layouts: 39 us -> none  [the longest x3 8.72 us: local(): jnp.take_along_axis((probs * chosen).T, source_rows, axis=1)]
  transfers between devices with their start and end apart: 34 -> 0, of which waited for: 20 -> 0; matrix products, arithmetic and copies ran while one was open for 10% -> 0% of each run, Pallas kernels for 0% -> 0%
where the time goes in v1:
time: 493 us; the launch traced here: 484 us
  Pallas kernels  308 us (62%)
  matrix products  98.2 us (20%)
  local copies, waits for them, and re-layouts  43.8 us (9%)
  other arithmetic  30.7 us (6%)
    pallas_call x1, Pallas kernels, scatter_all(): pl.pallas_call(functools.partial(scatter_kernel, depth, reach, cuts, per_...  114 us
    pallas_call x1, Pallas kernels, gather_all(): pl.pallas_call(functools.partial(gather_kernel, depth, reach, cuts), out_...  107 us
    pallas_call x1, Pallas kernels, give_back(): pl.pallas_call(functools.partial(return_kernel, n, groups), out_shape=(ha...  46.5 us
    pallas_call x1, Pallas kernels, dispatch(): pl.pallas_call(functools.partial(dispatch_kernel, n, owners), out_shape=(...  36.3 us
    dot_general x17, matrix products, matmul(): return jnp.dot(left, right, preferred_element_type=f32)  33.8 us
    dot_general x11, matrix products, input_grad(): lax.dot_general(left, right, (((1,), (1,)), ((), ())), preferred_element_...  24.4 us
    dot_general x11, matrix products, weight_grad(): lax.dot_general(left, right, (((0,), (0,)), ((), ())), preferred_element_...  24.2 us
    concatenate x3, local copies, waits for them, and re-layouts, local(): jnp.concatenate([grad_query, grad_key, grad_value, grad_out_t, grad_small...  14.2 us

profile of v1, /device:TPU:0, one launch (start us, length us, event | category | flops | bytes accessed | tf_op | source)
XLA Modules:
  0.0 483.6 jit_solution(786538368326791930)
XLA Ops:
  10.5 107.3 %gather_weights.1 = (bf16[4,2,2,48,4864]{4,3,2,1,0:T(8,128)(2,1)}, bf16[5,256,768]{2,1,0:T(8,128)(2,1)S(1)}) custom-call(bf16[48,4864]{1,0:T(8,128)(2,1)S(1)} %bitcast_dynamic-update-slice_fusion.shard, bf16[256,768]{1,0:T(8,128)(2,1)S(1)} %copy-done), custom_call_target="tpu_custom_call" | custom-call | tf_op jit(solution)/shard_map/gather_weights/pallas_call | solution.py:244
  121.5 3.1 convolution_convert_fusion.1
  125.3 1.8 multiply_convert_fusion.4
  129.3 2.6 fusion.115
  132.9 1.9 fusion.75
  136.5 1.9 exponential_reduce_fusion
  139.5 2.7 convolution_convert_fusion.13
  143.8 1.8 swap_cores.2
  146.7 2.1 fusion.16
  148.9 2.1 fusion.10
  151.1 3.5 multiply_convert_fusion.7
  155.9 1.6 convolution_convert_fusion.6
  162.2 2.9 multiply_convert_fusion.5
  165.2 36.3 %dispatch_rows.1 = (bf16[16,64,768]{2,1,0:T(8,128)(2,1)S(1)}, bf16[16,64,768]{2,1,0:T(8,128)(2,1)S(1)}) custom-call(bf16[16,64,768]{2,1,0:T(8,128)(2,1)S(1)} %bitcast.147, bf16[16,64,768]{2,1,0:T(8,128)(2,1)} %bitcast.189), custom_call_target="tpu_custom_call" | custom-call | tf_op jit(solution)/shard_map/dispatch_rows/pallas_call | solution.py:331
  201.5 1.8 fusion.59
  204.5 1.8 fusion.55
  206.4 4.7 multiply_convert_fusion.1
  211.1 4.9 %convolution_convert_fusion.5 = bf16[1024,768]{1,0:T(8,128)(2,1)S(1)} fusion(bf16[1024,1024]{1,0:T(8,128)(2,1)} %get-tuple-element.126, f32[1024,768]{1,0:T(8,128)S(1)} %copy-done.75), kind=kOutput, calls=%fused_computation.28 | convolution fusion | flops 1612185600 | bytes 6815744 | tf_op jit(solution)/shard_map/dot_general | solution.py:24
  216.1 1.8 fusion.57
  217.9 1.9 add_convert_fusion
  219.8 46.5 %return_rows.1 = (bf16[16,64,384]{2,1,0:T(8,128)(2,1)S(1)}, bf16[16,64,384]{2,1,0:T(8,128)(2,1)S(1)}) custom-call(bf16[16,64,768]{2,1,0:T(8,128)(2,1)S(1)} %bitcast.152, bf16[16,64,768]{2,1,0:T(8,128)(2,1)S(1)} %bitcast.153), custom_call_target="tpu_custom_call" | custom-call | tf_op jit(solution)/shard_map/return_rows/pallas_call | solution.py:404
  268.2 2.4 fusion.30.refs_0_
  270.6 2.2 fusion.8
  273.4 2.0 fusion.33.refs_1_
  276.2 2.5 swap_cores.3
  284.1 1.6 multiply_reduce_fusion.3
  285.8 2.5 convert_bitcast_fusion
  289.6 1.7 convolution_convert_fusion.12
  291.4 5.5 %multiply_reduce_fusion = (f32[6,256]{1,0:T(8,128)S(1)}, f32[6,256,1280]{2,1,0:T(8,128)S(1)}) fusion(f32[6,256,1280]{2,1,0:T(8,128)} %copy-done.7, f32[6,256]{1,0:T(8,128)S(1)} %copy-done.58, pred[256,1280]{1,0:T(8,128)(4,1)S(1)} %copy-done.15, bf16[256,6,64]{0,2,1:T(8,128)(2,1)S(1)} %bitcast.194, bf16[1280,6,64]{0,2,1:T(8,128)(2,1)} %bitcast.200), kind=kOutput, calls=%fused_computation.1 | convolution fusion | flops 259521024 | bytes 17248256 | tf_op jit(solution)/shard_map/qhe,khe->hqk/dot_general | solution.py:764
  297.3 2.2 multiply_convert_fusion
  302.7 4.0 copy.140
  306.8 3.1 convolution_bitcast_fusion
  310.2 2.0 convolution_convert_fusion.9
  312.3 1.9 convolution_convert_fusion
  315.1 2.0 convolution_convert_fusion.8
  317.1 1.9 copy.143
  319.0 2.2 convolution_convert_fusion.7
  323.3 2.4 fusion.72
  325.7 2.3 convolution_add_fusion
  330.0 1.9 copy-done.8
  334.3 1.7 convolution_convert_fusion.3
  336.0 1.8 convolution_convert_fusion.2
  337.9 12.1 %concatenate.77.grads = bf16[4,2,2,48,4864]{4,3,2,1,0:T(8,128)(2,1)} concatenate(bf16[4,2,2,48,384]{4,3,2,1,0:T(8,128)(2,1)} %convolution_convert_fusion.10, bf16[4,2,2,48,384]{4,3,2,1,0:T(8,128)(2,1)} %convolution_convert_fusion.9, bf16[4,2,2,48,384]{4,3,2,1,0:T(8,128)(2,1)} %convolution_convert_fusion.8, bf16[4,2,2,48,384]{4,3,2,1,0:T(8,128)(2,1)} %convolution_convert_fusion.7, ...), dimensions={4} | concatenate | bytes 14942208 | tf_op jit(solution)/shard_map/concatenate | solution.py:796
  350.1 2.3 convert_element_type.281.d_part
  352.4 114.1 %scatter_grads.1 = (f32[48,4864]{1,0:T(8,128)S(1)}, bf16[256,768]{1,0:T(8,128)(2,1)S(1)}) custom-call(bf16[4,2,2,48,4864]{4,3,2,1,0:T(8,128)(2,1)} %concatenate.77.grads, bf16[5,256,768]{2,1,0:T(8,128)(2,1)S(1)} %convert_element_type.281.d_part), custom_call_target="tpu_custom_call" | custom-call | tf_op jit(solution)/shard_map/scatter_grads/pallas_call | solution.py:551
  470.9 5.2 %fusion.116 = f32[768,1024]{1,0:T(8,128)} fusion(bf16[1024,768]{1,0:T(8,128)(2,1)S(1)} %bitcast.150, bf16[1024,1024]{1,0:T(8,128)(2,1)} %copy-done.31), kind=kOutput, calls=%fused_computation.214 | convolution fusion | flops 1610612736 | bytes 6815744 | tf_op jit(solution)/shard_map/dot_general | solution.py:28
  476.1 3.5 fusion.117
  479.6 3.6 fusion.118
  (266 shorter events, 55.2 us)
Async XLA Ops:
  119.2 6.1 %copy-start.61 = (f32[768]{0:T(1024)}, f32[768]{0:T(1024)S(1)}, u32[]{:S(2)}) copy-start(f32[768]{0:T(1024)S(1)} %convert_reduce_fusion.2) | copy-start | bytes 9220
  119.7 5.7 %copy-start.59 = (f32[5,256]{1,0:T(8,128)}, f32[5,256]{1,0:T(8,128)S(1)}, u32[]{:S(2)}) copy-start(f32[5,256]{1,0:T(8,128)S(1)} %add_rsqrt_fusion) | copy-start | bytes 15364
  121.5 3.1 copy-start.66
  125.3 13.1 %copy-start.14 = (pred[256,1280]{1,0:T(8,128)(4,1)}, pred[256,1280]{1,0:T(8,128)(4,1)S(1)}, u32[]{:S(2)}) copy-start(pred[256,1280]{1,0:T(8,128)(4,1)S(1)} %fusion.20) | copy-start | bytes 983044
  132.9 3.5 copy-start.21
  132.9 3.5 copy-start.23
  136.5 3.1 copy-start.7
  139.5 6.0 %copy-start.1 = (bf16[256,768]{1,0:T(8,128)(2,1)S(1)}, bf16[256,768]{1,0:T(8,128)(2,1)}, u32[]{:S(2)}) copy-start(bf16[256,768]{1,0:T(8,128)(2,1)} %tok.1) | copy-start | bytes 1179652
  142.2 4.4 copy-start.18
  146.5 4.6 copy-start.12
  146.5 4.6 copy-start.73
  148.9 5.7 %copy-start.10 = (bf16[256,768]{1,0:T(8,128)(2,1)}, bf16[256,768]{1,0:T(8,128)(2,1)S(1)}, u32[]{:S(2)}) copy-start(bf16[256,768]{1,0:T(8,128)(2,1)S(1)} %multiply_convert_fusion.9) | copy-start | bytes 1179652
  151.1 3.6 copy-start.69
  154.9 5.1 %copy-start.55 = (f32[256,16]{0,1:T(8,128)}, f32[256,16]{0,1:T(8,128)S(1)}, u32[]{:S(2)}) copy-start(f32[256,16]{0,1:T(8,128)S(1)} %fusion.85) | copy-start | bytes 49156
  162.2 39.3 %copy-start.76 = (f32[768,1024]{1,0:T(8,128)S(1)}, f32[768,1024]{1,0:T(8,128)}, u32[]{:S(2)}) copy-start(f32[768,1024]{1,0:T(8,128)} %param.29) | copy-start | bytes 9437188
  201.5 4.8 %copy-start.5 = (bf16[16,64,768]{2,1,0:T(8,128)(2,1)}, bf16[16,64,768]{2,1,0:T(8,128)(2,1)S(1)}, u32[]{:S(2)}) copy-start(bf16[16,64,768]{2,1,0:T(8,128)(2,1)S(1)} %get-tuple-element.29) | copy-start | bytes 4718596
  211.1 5.0 %copy-start.31 = (bf16[1024,1024]{1,0:T(8,128)(2,1)}, bf16[1024,1024]{1,0:T(8,128)(2,1)S(1)}, u32[]{:S(2)}) copy-start(bf16[1024,1024]{1,0:T(8,128)(2,1)S(1)} %get-tuple-element.125) | copy-start | bytes 6291460
  211.1 6.8 %copy-start.29 = (bf16[1024,1024]{1,0:T(8,128)(2,1)}, bf16[1024,1024]{1,0:T(8,128)(2,1)S(1)}, u32[]{:S(2)}) copy-start(bf16[1024,1024]{1,0:T(8,128)(2,1)S(1)} %get-tuple-element.124) | copy-start | bytes 6291460
  219.8 46.6 %copy-start.68 = (f32[256]{0:T(256)S(1)}, f32[256]{0:T(256)}, u32[]{:S(2)}) copy-start(f32[256]{0:T(256)} %copy-done.67) | copy-start | bytes 3076
  219.8 46.6 %copy-start.72 = (f32[256]{0:T(256)S(1)}, f32[256]{0:T(256)}, u32[]{:S(2)}) copy-start(f32[256]{0:T(256)} %copy-done.71) | copy-start | bytes 3076
  219.8 46.6 %copy-start.56 = (f32[256,16]{0,1:T(8,128)S(1)}, f32[256,16]{0,1:T(8,128)}, u32[]{:S(2)}) copy-start(f32[256,16]{0,1:T(8,128)} %copy-done.55) | copy-start | bytes 49156
  219.8 46.6 %copy-start.70 = (s32[256,2]{0,1:T(2,128)S(1)}, s32[256,2]{0,1:T(2,128)}, u32[]{:S(2)}) copy-start(s32[256,2]{0,1:T(2,128)} %param.32) | copy-start | bytes 6148
  219.8 47.1 %copy-start.19 = (bf16[256,768]{1,0:T(8,128)(2,1)S(1)}, bf16[256,768]{1,0:T(8,128)(2,1)}, u32[]{:S(2)}) copy-start(bf16[256,768]{1,0:T(8,128)(2,1)} %param.18) | copy-start | bytes 1179652
  281.9 3.9 copy-start.13
  285.8 5.6 %copy-start.15 = (pred[256,1280]{1,0:T(8,128)(4,1)S(1)}, pred[256,1280]{1,0:T(8,128)(4,1)}, u32[]{:S(2)}) copy-start(pred[256,1280]{1,0:T(8,128)(4,1)} %copy-done.14) | copy-start | bytes 983044
  285.8 5.6 %copy-start.58 = (f32[6,256]{1,0:T(8,128)S(1)}, f32[6,256]{1,0:T(8,128)}, u32[]{:S(2)}) copy-start(f32[6,256]{1,0:T(8,128)} %copy-done.57) | copy-start | bytes 18436
  291.4 5.5 %slice-start = ((s8[7864320]{0:T(1024)(128)(4,1)}), s8[4194304]{0:T(1024)(128)(4,1)S(1)}, s32[]{:S(2)}) async-start(s8[7864320]{0:T(1024)(128)(4,1)} %bitcast.159), calls=%async_computation | async-start | bytes 8388608
  291.4 5.9 %slice-start.1 = ((s8[7864320]{0:T(1024)(128)(4,1)}), s8[3670016]{0:T(1024)(128)(4,1)S(1)}, s32[]{:S(2)}) async-start(s8[7864320]{0:T(1024)(128)(4,1)} %bitcast.159), calls=%async_computation.1 | async-start | bytes 7340032
  300.9 5.8 %copy-start.36 = (f32[256,6,32]{0,2,1:T(8,128)S(1)}, f32[256,6,32]{0,2,1:T(8,128)}, u32[]{:S(2)}) copy-start(f32[256,6,32]{0,2,1:T(8,128)} %copy-done.35) | copy-start | bytes 589828
  300.9 5.8 %copy-start.38 = (f32[256,6,32]{0,2,1:T(8,128)S(1)}, f32[256,6,32]{0,2,1:T(8,128)}, u32[]{:S(2)}) copy-start(f32[256,6,32]{0,2,1:T(8,128)} %copy-done.37) | copy-start | bytes 589828
  301.5 8.4 %copy-start.33 = (bf16[256,6,64]{0,2,1:T(8,128)(2,1)}, bf16[256,6,64]{0,2,1:T(8,128)(2,1)S(1)}, u32[]{:S(2)}) copy-start(bf16[256,6,64]{0,2,1:T(8,128)(2,1)S(1)} %maximum_convert_fusion.1) | copy-start | bytes 589828
  302.7 7.1 %copy-start.40 = (f32[1280,32]{0,1:T(8,128)S(1)}, f32[1280,32]{0,1:T(8,128)}, u32[]{:S(2)}) copy-start(f32[1280,32]{0,1:T(8,128)} %copy-done.39) | copy-start | bytes 491524
  302.7 7.1 %copy-start.42 = (f32[1280,32]{0,1:T(8,128)S(1)}, f32[1280,32]{0,1:T(8,128)}, u32[]{:S(2)}) copy-start(f32[1280,32]{0,1:T(8,128)} %copy-done.41) | copy-start | bytes 491524
  306.8 3.5 copy-start.32
  306.8 5.5 %slice-start.2 = ((s8[7864320]{0:T(1024)(128)(4,1)}), s8[4194304]{0:T(1024)(128)(4,1)S(1)}, s32[]{:S(2)}) async-start(s8[7864320]{0:T(1024)(128)(4,1)} %bitcast.161), calls=%async_computation.2 | async-start | bytes 8388608
  314.2 4.9 %copy-start.46 = (bf16[6,64,256]{2,1,0:T(8,128)(2,1)S(1)}, bf16[6,64,256]{2,1,0:T(8,128)(2,1)}, u32[]{:S(2)}) copy-start(bf16[6,64,256]{2,1,0:T(8,128)(2,1)} %copy-done.45) | copy-start | bytes 589828
  315.1 6.2 %copy-start.11 = (bf16[256,768]{1,0:T(8,128)(2,1)S(1)}, bf16[256,768]{1,0:T(8,128)(2,1)}, u32[]{:S(2)}) copy-start(bf16[256,768]{1,0:T(8,128)(2,1)} %copy-done.10) | copy-start | bytes 1179652
  315.1 6.2 %copy-start.64 = (bf16[256,16]{0,1:T(8,128)(2,1)S(1)}, bf16[256,16]{0,1:T(8,128)(2,1)}, u32[]{:S(2)}) copy-start(bf16[256,16]{0,1:T(8,128)(2,1)} %copy-done.63) | copy-start | bytes 24580
  330.0 3.6 copy-start.50
  332.6 3.4 copy-start.20
  352.4 114.1 %copy-start.74 = (f32[256]{0:T(256)S(1)}, f32[256]{0:T(256)}, u32[]{:S(2)}) copy-start(f32[256]{0:T(256)} %get-tuple-element.149) | copy-start | bytes 3076
  352.4 114.1 %copy-start.2 = (bf16[256,768]{1,0:T(8,128)(2,1)S(1)}, bf16[256,768]{1,0:T(8,128)(2,1)}, u32[]{:S(2)}) copy-start(bf16[256,768]{1,0:T(8,128)(2,1)} %tok.1) | copy-start | bytes 1179652
  352.4 114.1 %copy-start.62 = (f32[768]{0:T(1024)S(1)}, f32[768]{0:T(1024)}, u32[]{:S(2)}) copy-start(f32[768]{0:T(1024)} %copy-done.61) | copy-start | bytes 9220
  352.4 114.4 %copy-start.16 = (f32[256,768]{1,0:T(8,128)S(1)}, f32[256,768]{1,0:T(8,128)}, u32[]{:S(2)}) copy-start(f32[256,768]{1,0:T(8,128)} %get-tuple-element.121) | copy-start | bytes 2359300
  466.5 4.4 copy-start.4
  470.9 5.2 %copy-start.30 = (bf16[1024,1024]{1,0:T(8,128)(2,1)S(1)}, bf16[1024,1024]{1,0:T(8,128)(2,1)}, u32[]{:S(2)}) copy-start(bf16[1024,1024]{1,0:T(8,128)(2,1)} %copy-done.29) | copy-start | bytes 6291460
  476.1 3.5 copy-start.6
  476.1 3.5 copy-start.78
  (35 other events, 64.0 us)

commit v2 on v1

--- a/solution.py
+++ b/solution.py
@@ -141,9 +141,9 @@
     half = tok.shape[0] // 2
     rows = pl.ds(pl.multiple_of(core * half, half), half)
     z_copies = []
-    t_copies = []
-    for c, (start, middle, stop) in enumerate(cuts):
-        cols = pl.ds(start, stop - start)
+
+    def start_first(c):
+        cols = pl.ds(cuts[c][0], cuts[c][2] - cuts[c][0])
         z_copies.append(
             [
                 push(
@@ -156,17 +156,19 @@
                 for k in range(depth - 1)
             ]
         )
-        if c == 0:
-            for k in range(reach):
-                t_copies.append(
-                    push(
-                        tok.at[rows],
-                        window.at[reach - 1 - k, rows],
-                        t_send.at[k],
-                        t_recv.at[k],
-                        ahead[k],
-                    )
-                )
+
+    start_first(0)
+    start_first(1)
+    t_copies = [
+        push(
+            tok.at[rows],
+            window.at[reach - 1 - k, rows],
+            t_send.at[k],
+            t_recv.at[k],
+            ahead[k],
+        )
+        for k in range(reach)
+    ]
     own_shard.wait()
     second, third, forwards = [], [], []
     for c in range(len(cuts) + 2):
@@ -193,7 +195,9 @@
                     ),
                 ]
             )
-        if c == 0:
+            if c + 2 < len(cuts):
+                start_first(c + 2)
+        if c == 1:
             for k, copy in enumerate(t_copies):
                 copy.wait_recv()
                 forwards.append(
@@ -228,15 +232,21 @@
                     ),
                 ]
             )
-    for copies in third:
-        for copy in copies:
-            copy.wait_recv()
+        if c >= 2:
+            for copy in third[c - 2]:
+                copy.wait_recv()
     for copy in forwards:
         copy.wait_recv()
     own_tok.wait()
     for copies in z_copies + second + third + [t_copies, forwards]:
         for copy in copies:
             copy.wait_send()
+
+
+def cut_columns(columns, parts):
+    step = 2 * LANES
+    edges = [step * (columns // step * i // parts) for i in range(parts + 1)]
+    return tuple((a, (a + b) // 2, b) for a, b in zip(edges[:-1], edges[1:]))
 
 
 def gather_all(shard, tokens, depth, reach, cuts):
@@ -412,164 +422,322 @@
     )(first, second)
 
 
-def scatter_kernel(
-    depth, reach, cuts, per_core, grads, d_part, total, d_full,
-    first_l, first_r, second_l, second_r, last, d_swap, d_sum, d_got, gain_got,
-    p_send, p_recv, z_send, z_recv, t_send, t_recv, f_send, f_recv,
+class Scatter:
+    def __init__(self, depth, chunks, total, buffers, semaphores):
+        self.depth, self.chunks, self.total = depth, chunks, total
+        self.first_l, self.first_r, self.second_l, self.second_r, self.last = buffers
+        self.p_send, self.p_recv, self.z_send, self.z_recv = semaphores
+        self.z, self.y, self.x = digits(lax.axis_index("dp"))
+        self.z_peers, self.y_peer, self.x_peer = grid_peers(depth, self.z, self.y, self.x)
+        self.at_l, self.at_r, l, r = [], [], 0, 0
+        for left, lc, lw, right, rc, rw, out in chunks:
+            self.at_l.append(pl.ds(l, lw))
+            self.at_r.append(pl.ds(r, rw))
+            l, r = l + lw, r + rw
+        self.ones, self.twos, self.threes = {}, {}, {}
+
+    def start(self, c):
+        left, lc, lw, right, rc, rw, out = self.chunks[c]
+        self.ones[c] = [
+            push(
+                left.at[:, :, 1 - self.x, :, pl.ds(lc, lw)],
+                self.first_l.at[:, :, :, self.at_l[c]],
+                self.p_send.at[c, 0], self.p_recv.at[c, 0], self.x_peer,
+            ),
+            push(
+                right.at[:, 1 - self.y, :, :, pl.ds(rc, rw)],
+                self.first_r.at[:, :, :, self.at_r[c]],
+                self.p_send.at[c, 1], self.p_recv.at[c, 1], self.y_peer,
+            ),
+        ]
+
+    def second(self, c):
+        left, lc, lw, right, rc, rw, out = self.chunks[c]
+        in_l, in_r, first_l, first_r = self.at_l[c], self.at_r[c], self.first_l, self.first_r
+        for copy in self.ones[c]:
+            copy.wait_recv()
+
+        def add(i, carry):
+            for j in range(2):
+                first_l[i, j, :, in_l] = (
+                    first_l[i, j, :, in_l].astype(f32) + left[i, j, self.x, :, pl.ds(lc, lw)].astype(f32)
+                ).astype(bf16)
+                first_r[i, j, :, in_r] = (
+                    first_r[i, j, :, in_r].astype(f32) + right[i, self.y, j, :, pl.ds(rc, rw)].astype(f32)
+                ).astype(bf16)
+            return carry
+
+        lax.fori_loop(0, self.depth, add, 0)
+        self.twos[c] = [
+            push(
+                first_l.at[:, 1 - self.y, :, in_l], self.second_l.at[:, :, in_l],
+                self.p_send.at[c, 2], self.p_recv.at[c, 2], self.y_peer,
+            ),
+            push(
+                first_r.at[:, 1 - self.x, :, in_r], self.second_r.at[:, :, in_r],
+                self.p_send.at[c, 3], self.p_recv.at[c, 3], self.x_peer,
+            ),
+        ]
+
+    def third(self, c):
+        for copy in self.twos[c]:
+            copy.wait_recv()
+        sides = (
+            (self.second_l, self.first_l, self.y, self.at_l[c]),
+            (self.second_r, self.first_r, self.x, self.at_r[c]),
+        )
+
+        def add(i, carry):
+            for source, before, place, here in sides:
+                source[i, :, here] = (
+                    source[i, :, here].astype(f32) + before[i, place, :, here].astype(f32)
+                ).astype(bf16)
+            return carry
+
+        lax.fori_loop(0, self.depth, add, 0)
+        self.threes[c] = [
+            push(
+                source.at[lax.rem(self.z + k + 1, self.depth), :, here],
+                self.last.at[k, side, :, here],
+                self.z_send.at[c, side, k], self.z_recv.at[c, side, k], self.z_peers[k],
+            )
+            for side, (source, before, place, here) in enumerate(sides)
+            for k in range(self.depth - 1)
+        ]
+
+    def finish(self, c):
+        left, lc, lw, right, rc, rw, out = self.chunks[c]
+        for copy in self.threes[c]:
+            copy.wait_recv()
+        for side, source, here, at, span in (
+            (0, self.second_l, self.at_l[c], out, lw),
+            (1, self.second_r, self.at_r[c], out + lw, rw),
+        ):
+            value = source[self.z, :, here].astype(f32)
+            for k in range(self.depth - 1):
+                value = value + self.last[k, side, :, here].astype(f32)
+            self.total[:, pl.ds(at, span)] = value
+
+    def drain(self):
+        for copies in list(self.ones.values()) + list(self.twos.values()) + list(self.threes.values()):
+            for copy in copies:
+                copy.wait_send()
+
+
+def lanes_of(part):
+    lane = lax.broadcasted_iota(jnp.int32, (1, LANES), 1)
+    return (lax.div(lane, HEAD) == part).astype(f32).astype(bf16)
+
+
+def swap_halves(values):
+    lane = lax.broadcasted_iota(jnp.int32, (1, LANES), 1)
+    low = lax.rem(lane, HEAD) < HEAD // 2
+    return jnp.where(
+        low, pltpu.roll(values, LANES - HEAD // 2, 1), pltpu.roll(values, HEAD // 2, 1)
+    )
+
+
+def put_rows(target, values, columns):
+    rows = target.shape[3]
+    for b in range(values.shape[0] // rows):
+        target[b // PLANE, (b // 2) % 2, b % 2, :, columns] = values[b * rows : (b + 1) * rows]
+
+
+def backward_kernel(
+    depth, reach, per_core, g_gate, g_up, g_down, g_small, window, q, k, v, lse, heads_out, d_attn,
+    query_w, key_w, value_w, out_t, gain, cosines, sines, bias, total, d_full,
+    grads, attn_t, d_heads, dq_all, dk_all, dv_all, d_part, d_swap, d_sum, d_got, gain_got,
+    first_l, first_r, second_l, second_r, last,
+    p_send, p_recv, z_send, z_recv, t_send, t_recv, s_send, s_recv, f_send, f_recv,
 ):
     n = depth * PLANE
     me, core = lax.axis_index("dp"), lax.axis_index("tensor")
-    z, y, x = digits(me)
-    z_peers, y_peer, x_peer = grid_peers(depth, z, y, x)
     sibling = {"tensor": 1 - core}
-    ahead = [{"dp": lax.rem(me + k, n)} for k in range(1, reach + 1)]
-    behind = [{"dp": lax.rem(me + n - k, n)} for k in range(1, reach + 1)]
-    greet(z_peers + [y_peer, x_peer, sibling] + ahead + behind)
+    ahead = [{"dp": lax.rem(me + i, n)} for i in range(1, reach + 1)]
+    behind = [{"dp": lax.rem(me + n - i, n)} for i in range(1, reach + 1)]
+    heads_width = q.shape[1]
+    count = q.shape[0]
+    pairs = heads_width // LANES
+    hidden = g_gate.shape[4]
+    chunks = []
+    out = 0
+    step = 2 * LANES
+    for source in (g_gate, g_up, g_down):
+        for at in range(0, hidden, 2 * step):
+            chunks.append((source, at, step, source, at + step, step, out))
+            out += 2 * step
+    early = len(chunks)
+    widths = [(step, step)] + [(step, LANES), (LANES, step)] * pairs
+    widths = widths[:pairs] + [(step, step)]
+    at = 0
+    for left, right in widths:
+        chunks.append((grads, at, left, grads, at + left, right, out + at))
+        at += left + right
+    scatter = Scatter(
+        depth, chunks, total, (first_l, first_r, second_l, second_r, last),
+        (p_send, p_recv, z_send, z_recv),
+    )
+    greet(scatter.z_peers + [scatter.y_peer, scatter.x_peer, sibling] + ahead + behind)
+    for c in range(3):
+        scatter.start(c)
+
+    d_heads[...] = matmul(d_attn[...], out_t[...]).astype(bf16)
+    put_rows(grads, weight_grad(d_attn[...], heads_out[...]).astype(bf16), pl.ds(0, heads_width))
+    grads[:, :, :, :, pl.ds(heads_width, LANES)] = g_small[...]
+
+    def normed(block):
+        values = window[block].astype(f32)
+        return values * lax.rsqrt(jnp.mean(values * values, axis=-1, keepdims=True) + eps)
+
+    def turned(block, carry):
+        rows = pl.ds(pl.multiple_of(block * count, count), count)
+        attn_t[:, rows] = (normed(block) * gain[...]).T.astype(bf16)
+        return carry
+
+    for block in range(reach + 1):
+        turned(block, 0)
+    scatter.start(early)
+    own = pl.ds(reach * count, count)
+    done = 0
+    for pair in range(pairs):
+        columns = pl.ds(pair * LANES, LANES)
+        k_pair, v_pair, q_pair, d_pair = k[:, columns], v[:, columns], q[:, columns], d_heads[:, columns]
+        dq = dk = dv = None
+        for part in range(2):
+            head = 2 * pair + part
+            lanes = lanes_of(part)
+            q_head, d_head, k_head = q_pair * lanes, d_pair * lanes, k_pair * lanes
+            probs = jnp.exp(input_grad(k_pair, q_head) + bias[...] - lse[head : head + 1, :])
+            d_probs = input_grad(v_pair, d_head)
+            inner = jnp.sum(probs * d_probs, axis=0, keepdims=True)
+            d_scores = (probs * (d_probs - inner)).astype(bf16)
+            parts = (
+                weight_grad(d_scores, k_head),
+                matmul(d_scores, q_head),
+                matmul(probs.astype(bf16), d_head),
+            )
+            dq, dk, dv = parts if part == 0 else (dq + parts[0], dk + parts[1], dv + parts[2])
+            if done < early + 1:
+                scatter.second(done)
+                if done + 3 < early:
+                    scatter.start(done + 3)
+            if 1 <= done:
+                scatter.third(done - 1)
+            if 2 <= done:
+                scatter.finish(done - 2)
+            done += 1
+        dq = dq * (HEAD ** (-0.5))
+        cos_own, sin_own = cosines[own, :], sines[own, :]
+        dq_low = (dq * cos_own - swap_halves(dq) * sin_own).astype(bf16)
+        dk_low = (dk * cosines[...] - swap_halves(dk) * sines[...]).astype(bf16)
+        dv_low = dv.astype(bf16)
+        dq_all[:, columns] = dq_low
+        dk_all[:, columns] = dk_low
+        dv_all[:, columns] = dv_low
+        at = heads_width + LANES + pair * 3 * LANES
+        put_rows(grads, matmul(attn_t[:, own], dq_low).astype(bf16), pl.ds(at, LANES))
+        put_rows(grads, matmul(attn_t[...], dk_low).astype(bf16), pl.ds(at + LANES, LANES))
+        put_rows(grads, matmul(attn_t[...], dv_low).astype(bf16), pl.ds(at + 2 * LANES, LANES))
+        if pair < pairs - 1:
+            scatter.start(early + 1 + pair)
+
     width = d_part.shape[-1] // 2
     mine = pl.ds(pl.multiple_of(core * width, width), width)
     theirs = pl.ds(pl.multiple_of((1 - core) * width, width), width)
-    swapped = push(d_part.at[:, :, theirs], d_swap, f_send.at[0], f_recv.at[0], sibling)
-    ones = []
-    for c, (start, middle, stop) in enumerate(cuts):
-        left, right = pl.ds(start, middle - start), pl.ds(middle, stop - middle)
-        ones.append(
-            [
-                push(
-                    grads.at[:, :, 1 - x, :, left],
-                    first_l.at[:, :, :, pl.ds(start // 2, middle - start)],
-                    p_send.at[c, 0], p_recv.at[c, 0], x_peer,
-                ),
-                push(
-                    grads.at[:, 1 - y, :, :, right],
-                    first_r.at[:, :, :, pl.ds(start // 2, stop - middle)],
-                    p_send.at[c, 1], p_recv.at[c, 1], y_peer,
-                ),
-            ]
+    swaps = []
+    gain_row = jnp.zeros((1, 2 * width), f32)
+    for block in range(reach + 1):
+        rows = pl.ds(block * count, count)
+        value = input_grad(dk_all[rows, :], key_w[...]) + input_grad(dv_all[rows, :], value_w[...])
+        if block == reach:
+            value = value + input_grad(dq_all[...], query_w[...])
+        gain_row = gain_row + jnp.sum(value * normed(block), axis=0, keepdims=True)
+        d_part[block] = value.astype(bf16)
+        swaps.append(
+            push(
+                d_part.at[block, :, theirs], d_swap.at[block],
+                s_send.at[block], s_recv.at[block], sibling,
+            )
         )
-    swapped.wait_recv()
-    d_sum[...] = (d_part[:, :, mine].astype(f32) + d_swap[...].astype(f32)).astype(bf16)
-    back = [
-        push(d_sum.at[reach - 1 - k], d_got.at[k], t_send.at[k], t_recv.at[k], behind[k])
-        for k in range(reach)
-    ]
-    twos, threes = [], []
-    for c in range(len(cuts) + 2):
-        if c < len(cuts):
-            start, middle, stop = cuts[c]
-            span = middle - start
-            left, right = pl.ds(start, span), pl.ds(middle, span)
-            here = pl.ds(start // 2, span)
-            for copy in ones[c]:
-                copy.wait_recv()
-
-            def add_first(i, carry):
-                for j in range(2):
-                    first_l[i, j, :, here] = (
-                        first_l[i, j, :, here].astype(f32) + grads[i, j, x, :, left].astype(f32)
-                    ).astype(bf16)
-                    first_r[i, j, :, here] = (
-                        first_r[i, j, :, here].astype(f32) + grads[i, y, j, :, right].astype(f32)
-                    ).astype(bf16)
-                return carry
-
-            lax.fori_loop(0, depth, add_first, 0)
-            twos.append(
-                [
-                    push(
-                        first_l.at[:, 1 - y, :, here], second_l.at[:, :, here],
-                        p_send.at[c, 2], p_recv.at[c, 2], y_peer,
-                    ),
-                    push(
-                        first_r.at[:, 1 - x, :, here], second_r.at[:, :, here],
-                        p_send.at[c, 3], p_recv.at[c, 3], x_peer,
-                    ),
-                ]
+    put_rows(
+        grads,
+        jnp.broadcast_to(gain_row, (LANES, 2 * width)).T.astype(bf16),
+        pl.ds(heads_width + LANES + pairs * 3 * LANES, LANES),
+    )
+    final = len(chunks) - 1
+    scatter.start(final)
+    back = []
+    for block in range(reach + 1):
+        swaps[block].wait_recv()
+        d_sum[block] = (
+            d_part[block, :, mine].astype(f32) + d_swap[block].astype(f32)
+        ).astype(bf16)
+        if block < reach:
+            i = reach - 1 - block
+            back.append(
+                push(d_sum.at[block], d_got.at[i], t_send.at[i], t_recv.at[i], behind[i])
             )
-        if 1 <= c <= len(cuts):
-            start, middle, stop = cuts[c - 1]
-            span = middle - start
-            here = pl.ds(start // 2, span)
-            for copy in twos[c - 1]:
-                copy.wait_recv()
-
-            def add_second(i, carry):
-                second_l[i, :, here] = (
-                    second_l[i, :, here].astype(f32) + first_l[i, y, :, here].astype(f32)
-                ).astype(bf16)
-                second_r[i, :, here] = (
-                    second_r[i, :, here].astype(f32) + first_r[i, x, :, here].astype(f32)
-                ).astype(bf16)
-                return carry
-
-            lax.fori_loop(0, depth, add_second, 0)
-            threes.append(
-                [
-                    push(
-                        source.at[lax.rem(z + k + 1, depth), :, here],
-                        last.at[k, side, :, here],
-                        z_send.at[c - 1, side, k], z_recv.at[c - 1, side, k], z_peers[k],
-                    )
-                    for side, source in ((0, second_l), (1, second_r))
-                    for k in range(depth - 1)
-                ]
-            )
-        if c >= 2:
-            start, middle, stop = cuts[c - 2]
-            span = middle - start
-            here = pl.ds(start // 2, span)
-            for copy in threes[c - 2]:
-                copy.wait_recv()
-            for side, source, at in ((0, second_l, start), (1, second_r, middle)):
-                value = source[z, :, here].astype(f32)
-                for k in range(depth - 1):
-                    value = value + last[k, side, :, here].astype(f32)
-                total[:, pl.ds(at, span)] = value
+    seconds = [c for c in range(len(chunks)) if c not in scatter.twos]
+    for c in range(done - 1, len(chunks) + 2):
+        if c < len(chunks) and c not in scatter.twos:
+            scatter.second(c)
+        if c - 1 < len(chunks) and c - 1 not in scatter.threes:
+            scatter.third(c - 1)
+        if c >= 2 and c - 2 >= done - 2:
+            scatter.finish(c - 2)
     d_mine = d_sum[reach].astype(f32)
-    for k, copy in enumerate(back):
+    for copy in back:
         copy.wait_recv()
-        d_mine = d_mine + d_got[k].astype(f32)
+    for i in range(reach):
+        d_mine = d_mine + d_got[i].astype(f32)
     d_full[:, mine] = d_mine.astype(bf16)
-    both = push(d_full.at[:, mine], d_full.at[:, mine], f_send.at[1], f_recv.at[1], sibling)
+    both = push(d_full.at[:, mine], d_full.at[:, mine], f_send.at[0], f_recv.at[0], sibling)
     split = pl.ds(per_core, LANES)
-    gain = push(total.at[:, split], gain_got, f_send.at[2], f_recv.at[2], sibling)
-    both.wait_recv()
-    gain.wait()
+    gain_copy = push(total.at[:, split], gain_got, f_send.at[1], f_recv.at[1], sibling)
+    both.wait()
+    gain_copy.wait()
     total[:, split] = total[:, split] + gain_got[...]
-    for copies in ones + twos + threes + [back, [swapped, both]]:
-        for copy in copies:
-            copy.wait_send()
-
-
-def scatter_all(grads, d_part, per_core, depth, reach, cuts):
-    rows, columns = grads.shape[0] // (depth * PLANE), grads.shape[1]
-    grads = grads.reshape(depth, 2, 2, rows, columns)
-    count, width = d_part.shape[0] // (reach + 1), d_part.shape[1]
-    d_part = d_part.reshape(reach + 1, count, width)
-    parts, half = len(cuts), columns // 2
+    scatter.drain()
+    for copy in back + swaps:
+        copy.wait_send()
+
+
+def backward(arrays, rows, columns, shared, count, heads_width, width, depth, reach):
+    span = (reach + 1) * count
+    half = columns // 2
+    parts = shared // (4 * LANES) + 2 + heads_width // LANES
     first = pltpu.VMEM((depth, 2, rows, half), bf16)
     second = pltpu.VMEM((depth, rows, half), bf16)
+    own = columns - shared
     return pl.pallas_call(
-        functools.partial(scatter_kernel, depth, reach, cuts, per_core),
+        functools.partial(backward_kernel, depth, reach, columns - LANES),
         out_shape=(
             jax.ShapeDtypeStruct((rows, columns), f32),
             jax.ShapeDtypeStruct((count, width), bf16),
         ),
-        in_specs=[IN_VMEM] * 2,
+        in_specs=[IN_VMEM] * len(arrays),
         out_specs=(IN_VMEM, IN_VMEM),
         scratch_shapes=[
-            first, first, second, second,
-            pltpu.VMEM((depth - 1, 2, rows, half), bf16),
+            pltpu.VMEM((depth, 2, 2, rows, own), bf16),
+            pltpu.VMEM((width, span), bf16),
+            pltpu.VMEM((count, heads_width), bf16),
+            pltpu.VMEM((count, heads_width), bf16),
+            pltpu.VMEM((span, heads_width), bf16),
+            pltpu.VMEM((span, heads_width), bf16),
+            pltpu.VMEM((reach + 1, count, width), bf16),
             pltpu.VMEM((reach + 1, count, width // 2), bf16),
             pltpu.VMEM((reach + 1, count, width // 2), bf16),
             pltpu.VMEM((reach, count, width // 2), bf16),
             pltpu.VMEM((rows, LANES), f32),
+            first, first, second, second,
+            pltpu.VMEM((depth - 1, 2, rows, half), bf16),
             dma(parts, 4), dma(parts, 4),
             dma(parts, 2, depth - 1), dma(parts, 2, depth - 1),
-            dma(reach), dma(reach), dma(3), dma(3),
+            dma(reach), dma(reach), dma(reach + 1), dma(reach + 1), dma(2), dma(2),
         ],
-        compiler_params=comm_params(4),
-        name="scatter_grads",
-    )(grads, d_part)
+        compiler_params=comm_params(4, 58 << 20),
+        name="attention_backward",
+    )(*arrays)
 
 
 def local(
@@ -607,8 +775,7 @@
     at_small = 4 * heads_width
     at_shared = at_small + small
     columns = at_shared + 3 * hidden
-    edges = [0, at_small, at_shared + hidden, at_shared + 2 * hidden, columns]
-    cuts = tuple((a, (a + b) // 2, b) for a, b in zip(edges[:-1], edges[1:]))
+    cuts = cut_columns(columns, 7)
     full, window = gather_all(packed, tokens, depth, reach, cuts)
     query_w = full[:, :heads_width]
     key_w = full[:, heads_width : 2 * heads_width]
@@ -757,47 +924,50 @@
         d_norm_two - normed_two * jnp.mean(d_norm_two * normed_two, axis=-1, keepdims=True)
     )
 
-    d_attn = d_middle.astype(bf16)
-    grad_out_t = weight_grad(d_attn, heads_out)
-    d_heads = matmul(d_attn, out_t).astype(bf16).reshape(head_shape)
-    again = jnp.exp(masked_scores(queries, all_keys, valid) - lse)
-    d_weights = jnp.einsum("qhe,khe->hqk", d_heads, all_values, preferred_element_type=f32)
-    d_scores = (again * (d_weights - jnp.sum(again * d_weights, axis=-1, keepdims=True))).astype(bf16)
-    d_queries = (
-        jnp.einsum("hqk,khe->qhe", d_scores, all_keys, preferred_element_type=f32) * score_scale
-    )
-    d_keys = jnp.einsum("hqk,qhe->khe", d_scores, queries, preferred_element_type=f32)
-    d_values = jnp.einsum("hqk,qhe->khe", again.astype(bf16), d_heads, preferred_element_type=f32)
-    d_query_pre = unrotate(d_queries, cosines, sines).astype(bf16).reshape(tok_count, -1)
-    d_key_pre = unrotate(d_keys, cos_all, sin_all).astype(bf16).reshape(span, -1)
-    d_value_pre = d_values.astype(bf16).reshape(span, -1)
-    grad_query = weight_grad(attn_in, d_query_pre)
-    grad_key = weight_grad(attn_in_all, d_key_pre)
-    grad_value = weight_grad(attn_in_all, d_value_pre)
-    d_attn_part = input_grad(d_key_pre, key_w) + input_grad(d_value_pre, value_w)
-    d_attn_part = jnp.concatenate(
+    cos_wide = jnp.tile(cos_all[:, 0, :], (1, 4))
+    sin_wide = jnp.tile(sin_all[:, 0, :], (1, 4)) * jnp.where(
+        jnp.arange(LANES) % HEAD < HEAD // 2, -1.0, 1.0
+    )
+    bias = jnp.where(valid.T, 0.0, masked).astype(f32)
+    lse_rows = jnp.pad(lse[:, :, 0], ((0, -local_heads % 8), (0, 0)))
+    blocks = (depth, 2, 2, shard_rows)
+    grad_small = jnp.concatenate(
+        [grad_router, grad_gain_two[:, None], jnp.zeros((width, LANES - experts - 1), f32)], axis=1
+    ).astype(bf16)
+    total, d_attn_in = backward(
         [
-            d_attn_part[: reach * tok_count],
-            d_attn_part[reach * tok_count :] + input_grad(d_query_pre, query_w),
+            grad_sgate.astype(bf16).reshape(blocks + (hidden,)),
+            grad_sup.astype(bf16).reshape(blocks + (hidden,)),
+            grad_sdown_t.astype(bf16).reshape(blocks + (hidden,)),
+            grad_small.reshape(blocks + (LANES,)),
+            window.reshape(reach + 1, tok_count, width),
+            queries.reshape(tok_count, -1),
+            all_keys.reshape(span, -1),
+            all_values.reshape(span, -1),
+            lse_rows,
+            heads_out,
+            d_middle.astype(bf16),
+            query_w, key_w, value_w, out_t,
+            gain_first[None, :],
+            cos_wide, sin_wide, bias,
         ],
-        axis=0,
-    )
-    grad_gain_one = jnp.sum(d_attn_part * normed_all, axis=0)
-    grad_small = jnp.concatenate(
-        [
-            grad_router,
-            grad_gain_two[:, None],
-            jnp.zeros((width, LANES - experts - 1), f32),
-            grad_gain_one[:, None],
-            jnp.zeros((width, small - LANES - 1), f32),
-        ],
-        axis=1,
-    )
-    grads = jnp.concatenate(
-        [grad_query, grad_key, grad_value, grad_out_t, grad_small, grad_sgate, grad_sup, grad_sdown_t],
-        axis=1,
-    ).astype(bf16)
-    total, d_attn_in = scatter_all(grads, d_attn_part.astype(bf16), at_small + LANES, depth, reach, cuts)
+        shard_rows, columns, 3 * hidden, tok_count, heads_width, width, depth, reach,
+    )
+    def columns_of(at, count):
+        return total[:, at : at + count]
+
+    at_out = 3 * hidden
+    at_pairs = at_out + heads_width + LANES
+    grad_parts = [
+        jnp.concatenate(
+            [
+                columns_of(at_pairs + (3 * pair + i) * LANES, LANES)
+                for pair in range(heads_width // LANES)
+            ],
+            axis=1,
+        )
+        for i in range(3)
+    ]
     d_attn_in = d_attn_in.astype(f32)
     d_norm_one = d_attn_in * gain_first
     token_input_gradient = d_middle + scale_one * (
@@ -806,16 +976,16 @@
     return (
         output,
         token_input_gradient,
-        total[:, at_small + LANES],
-        total[:, :heads_width],
-        total[:, heads_width : 2 * heads_width],
-        total[:, 2 * heads_width : 3 * heads_width],
-        total[:, 3 * heads_width : at_small].T,
-        total[:, at_small + experts],
-        total[:, at_small : at_small + experts],
-        total[:, at_shared : at_shared + hidden],
-        total[:, at_shared + hidden : at_shared + 2 * hidden],
-        total[:, at_shared + 2 * hidden :].T,
+        total[:, columns - LANES],
+        grad_parts[0],
+        grad_parts[1],
+        grad_parts[2],
+        columns_of(at_out, heads_width).T,
+        total[:, at_out + heads_width + experts],
+        columns_of(at_out + heads_width, experts),
+        columns_of(0, hidden),
+        columns_of(hidden, hidden),
+        columns_of(2 * hidden, hidden).T,
         grad_e_gate,
         grad_e_up,
         grad_e_down,

time: 493 us -> 438 us (0.89)
  matrix products: 98.2 us -> 71.6 us
  local copies, waits for them, and re-layouts: 43.8 us -> 25.7 us
  Pallas kernels: 308 us -> 298 us
    concatenate x3 -> x2, local copies, waits for them, and re-layouts: 14.2 us -> 0.43 us  [local(): jnp.concatenate([grad_router, grad_gain_two[:, None], jnp.zeros((width, L...]
    dot_general x4 -> x0, matrix products: 11.8 us -> none  [the longest x1 5.5 us: local(): jnp.einsum('qhe,khe->hqk', d_heads, all_values, preferred_element_type=f32)]
    pallas_call x1, Pallas kernels: 107 us -> 95.6 us  [gather_all(): pl.pallas_call(functools.partial(gather_kernel, depth, reach, cuts), out_...]
    dot_general x4 -> x0, local copies, waits for them, and re-layouts: 7.15 us -> none  [weight_grad(): lax.dot_general(left, right, (((0,), (0,)), ((), ())), preferred_element_...]
    dot_general x11 -> x7, matrix products: 24.2 us -> 17.1 us  [weight_grad(): lax.dot_general(left, right, (((0,), (0,)), ((), ())), preferred_element_...]
    unnamed x169 -> x125, local copies, waits for them, and re-layouts: 12 us -> 5.65 us
    dot_general x11 -> x8, matrix products: 24.4 us -> 18.6 us  [input_grad(): lax.dot_general(left, right, (((1,), (1,)), ((), ())), preferred_element_...]
    dot_general x17 -> x16, matrix products: 33.8 us -> 29.5 us  [matmul(): return jnp.dot(left, right, preferred_element_type=f32)]
where the time goes in v2:
time: 438 us; the launch traced here: 430 us
  Pallas kernels  298 us (68%)
  matrix products  71.6 us (16%)
  other arithmetic  31.9 us (7%)
  local copies, waits for them, and re-layouts  25.7 us (6%)
    pallas_call x1, Pallas kernels, backward(): pl.pallas_call(functools.partial(backward_kernel, depth, reach, columns -...  116 us
    pallas_call x1, Pallas kernels, gather_all(): pl.pallas_call(functools.partial(gather_kernel, depth, reach, cuts), out_...  95.6 us
    pallas_call x1, Pallas kernels, give_back(): pl.pallas_call(functools.partial(return_kernel, n, groups), out_shape=(ha...  45.8 us
    pallas_call x1, Pallas kernels, dispatch(): pl.pallas_call(functools.partial(dispatch_kernel, n, owners), out_shape=(...  36.9 us
    dot_general x16, matrix products, matmul(): return jnp.dot(left, right, preferred_element_type=f32)  29.5 us
    dot_general x8, matrix products, input_grad(): lax.dot_general(left, right, (((1,), (1,)), ((), ())), preferred_element_...  18.6 us
    dot_general x7, matrix products, weight_grad(): lax.dot_general(left, right, (((0,), (0,)), ((), ())), preferred_element_...  17.1 us

profile of v2, /device:TPU:0, one launch (start us, length us, event | category | flops | bytes accessed | tf_op | source)
XLA Modules:
  0.0 429.6 jit_solution(16863937641602253024)
XLA Ops:
  10.5 95.6 %gather_weights.1 = (bf16[4,2,2,48,4864]{4,3,2,1,0:T(8,128)(2,1)}, bf16[5,256,768]{2,1,0:T(8,128)(2,1)S(1)}) custom-call(bf16[48,4864]{1,0:T(8,128)(2,1)S(1)} %bitcast_dynamic-update-slice_fusion.shard, bf16[256,768]{1,0:T(8,128)(2,1)S(1)} %copy-done.1), custom_call_target="tpu_custom_call" | custom-call | tf_op jit(solution)/shard_map/gather_weights/pallas_call | solution.py:254
  106.1 1.8 convert_reduce_fusion
  109.0 1.3 copy-done.12
  110.2 1.5 fusion.77
  113.3 1.8 multiply_convert_fusion.3
  115.2 3.3 fusion.100
  119.5 2.1 fusion.105
  121.9 1.4 select_reduce_fusion
  123.4 1.9 exponential_reduce_fusion
  125.2 1.4 copy-done.3
  126.7 2.3 convolution_convert_fusion.v
  129.9 4.9 %fusion.42 = bf16[6,64,256]{2,1,0:T(8,128)(2,1)S(1)} fusion(bf16[1280,6,64]{0,2,1:T(8,128)(2,1)S(1)} %bitcast.142, f32[6,256,1280]{2,1,0:T(8,128)} %copy-done.3, f32[6,256]{1,0:T(8,128)S(1)} %log_add_fusion, pred[256,1280]{1,0:T(8,128)(4,1)S(1)} %fusion.23), kind=kOutput, calls=%fused_computation.56 | convolution fusion | flops 257654784 | bytes 9377792 | tf_op jit(solution)/shard_map/hqk,khe->qhe/dot_general | solution.py:823
  134.9 1.5 convolution_convert_fusion.6.refs_0_
  136.5 1.8 swap_cores.2
  141.5 1.7 multiply_convert_fusion.4
  143.8 36.9 %dispatch_rows.1 = (bf16[16,64,768]{2,1,0:T(8,128)(2,1)S(1)}, bf16[16,64,768]{2,1,0:T(8,128)(2,1)S(1)}) custom-call(bf16[16,64,768]{2,1,0:T(8,128)(2,1)S(1)} %bitcast.108, bf16[16,64,768]{2,1,0:T(8,128)(2,1)} %bitcast.136), custom_call_target="tpu_custom_call" | custom-call | tf_op jit(solution)/shard_map/dispatch_rows/pallas_call | solution.py:341
  180.8 3.8 fusion.61
  184.7 1.8 fusion.65
  186.5 4.1 multiply_convert_fusion
  190.7 3.6 fusion.108
  194.2 3.5 fusion.107
  197.7 3.5 fusion.106
  201.9 1.8 fusion.63
  203.8 1.8 add_convert_fusion
  205.6 1.8 convolution_convert_fusion.4
  207.4 45.8 %return_rows.1 = (bf16[16,64,384]{2,1,0:T(8,128)(2,1)S(1)}, bf16[16,64,384]{2,1,0:T(8,128)(2,1)S(1)}) custom-call(bf16[16,64,768]{2,1,0:T(8,128)(2,1)S(1)} %bitcast.114, bf16[16,64,768]{2,1,0:T(8,128)(2,1)S(1)} %bitcast.113), custom_call_target="tpu_custom_call" | custom-call | tf_op jit(solution)/shard_map/return_rows/pallas_call | solution.py:414
  255.0 2.2 fusion.75
  257.4 1.9 fusion.68
  259.3 2.0 fusion.13
  261.3 2.0 fusion.19
  263.3 3.2 multiply_convert_fusion.6
  266.5 3.3 fusion.11
  269.8 2.5 fusion.39.refs_1_
  272.4 2.0 fusion.36.refs_0_
  274.5 2.5 swap_cores.3
  277.2 1.4 multiply_reduce_fusion.2
  279.5 2.0 fusion.99.d_attn
  283.1 1.7 convolution_convert_fusion.2
  284.9 2.9 convolution_convert_fusion.3
  287.7 1.8 convolution_convert_fusion.1
  291.0 2.1 maximum_convert_fusion
  293.1 2.3 copy.127.k
  296.2 1.9 fusion.26.bias
  299.6 1.3 copy.125
  303.1 115.7 %attention_backward.1 = (f32[48,4864]{1,0:T(8,128)}, bf16[256,768]{1,0:T(8,128)(2,1)}) custom-call(bf16[4,2,2,48,1024]{4,3,2,1,0:T(8,128)(2,1)} %bitcast.134, bf16[4,2,2,48,1024]{4,3,2,1,0:T(8,128)(2,1)} %bitcast.133, bf16[4,2,2,48,1024]{4,3,2,1,0:T(8,128)(2,1)} %bitcast.135, bf16[4,2,2,48,128]{4,3,2,1,0:T(8,128)(2,1)} %maximum_maximum_fusion.g_small, ...), custom_call_target="tpu_custom_call" | custom-call | tf_op jit(solution)/shard_map/attention_backward/pallas_call | solution.py:712
  421.7 1.3 fusion.52
  423.0 2.6 fusion.55
  427.7 1.5 slice_reduce_fusion
  (210 shorter events, 34.6 us)
Async XLA Ops:
  106.1 7.2 %copy-start = (bf16[5,256,768]{2,1,0:T(8,128)(2,1)}, bf16[5,256,768]{2,1,0:T(8,128)(2,1)S(1)}, u32[]{:S(2)}) copy-start(bf16[5,256,768]{2,1,0:T(8,128)(2,1)S(1)} %get-tuple-element.26.window) | copy-start | bytes 5898244
  107.9 5.4 %copy-start.31 = (f32[768]{0:T(1024)}, f32[768]{0:T(1024)S(1)}, u32[]{:S(2)}) copy-start(f32[768]{0:T(1024)S(1)} %get-tuple-element.113) | copy-start | bytes 9220
  107.9 31.2 %copy-start.33 = (f32[768]{0:T(1024)}, f32[768]{0:T(1024)S(1)}, u32[]{:S(2)}) copy-start(f32[768]{0:T(1024)S(1)} %get-tuple-element.112) | copy-start | bytes 9220
  111.7 3.4 copy-start.37
  112.4 2.7 copy-start.17
  112.4 2.7 copy-start.20
  112.5 9.4 %copy-start.15 = (bf16[256,6,64]{0,2,1:T(8,128)(2,1)}, bf16[256,6,64]{0,2,1:T(8,128)(2,1)S(1)}, u32[]{:S(2)}) copy-start(bf16[256,6,64]{0,2,1:T(8,128)(2,1)S(1)} %fusion.79) | copy-start | bytes 589828
  112.6 2.5 copy-start.52
  112.6 2.5 copy-start.54
  112.7 2.4 copy-start.35
  112.7 2.4 copy-start.50
  115.2 4.4 %copy-start.14 = (bf16[5,256,768]{2,1,0:T(8,128)(2,1)S(1)}, bf16[5,256,768]{2,1,0:T(8,128)(2,1)}, u32[]{:S(2)}) copy-start(bf16[5,256,768]{2,1,0:T(8,128)(2,1)} %multiply_convert_fusion.3) | copy-start | bytes 5898244
  123.3 3.3 copy-start.3
  123.3 3.3 copy-start.13
  126.7 3.2 copy-start.44
  134.9 3.3 copy-start.2
  138.2 3.3 copy-start.4
  140.5 60.7 %copy-start.40 = (f32[256]{0:T(256)}, f32[256]{0:T(256)S(1)}, u32[]{:S(2)}) copy-start(f32[256]{0:T(256)S(1)} %get-tuple-element.163) | copy-start | bytes 3076
  140.5 60.7 %copy-start.46 = (f32[256]{0:T(256)}, f32[256]{0:T(256)S(1)}, u32[]{:S(2)}) copy-start(f32[256]{0:T(256)S(1)} %fusion.91) | copy-start | bytes 3076
  180.8 3.9 copy-start.58
  201.9 51.3 %copy-start.57 = (s32[256,1]{0,1:T(1,128)}, s32[256,1]{0,1:T(1,128)S(1)}, u32[]{:S(2)}) copy-start(s32[256,1]{0,1:T(1,128)S(1)} %get-tuple-element.160) | copy-start | bytes 3076
  266.5 3.3 copy-start.29
  266.5 5.8 %copy-start.28 = (bf16[256,1024]{1,0:T(8,128)(2,1)}, bf16[256,1024]{1,0:T(8,128)(2,1)S(1)}, u32[]{:S(2)}) copy-start(bf16[256,1024]{1,0:T(8,128)(2,1)S(1)} %get-tuple-element.134) | copy-start | bytes 1572868
  269.8 2.5 copy-start.26
  269.8 2.6 copy-start.61
  272.4 4.7 %copy-start.43 = (s32[256,2]{0,1:T(2,128)S(1)}, s32[256,2]{0,1:T(2,128)}, u32[]{:S(2)}) copy-start(s32[256,2]{0,1:T(2,128)} %param.32) | copy-start | bytes 6148
  272.4 4.8 %copy-start.41 = (f32[256]{0:T(256)S(1)}, f32[256]{0:T(256)}, u32[]{:S(2)}) copy-start(f32[256]{0:T(256)} %copy-done.40) | copy-start | bytes 3076
  272.4 4.8 %copy-start.47 = (f32[256]{0:T(256)S(1)}, f32[256]{0:T(256)}, u32[]{:S(2)}) copy-start(f32[256]{0:T(256)} %copy-done.46) | copy-start | bytes 3076
  272.4 4.8 %copy-start.34 = (f32[768]{0:T(1024)S(1)}, f32[768]{0:T(1024)}, u32[]{:S(2)}) copy-start(f32[768]{0:T(1024)} %copy-done.33) | copy-start | bytes 9220
  272.4 4.8 %copy-start.49 = (f32[256]{0:T(256)S(1)}, f32[256]{0:T(256)}, u32[]{:S(2)}) copy-start(f32[256]{0:T(256)} %copy-done.48) | copy-start | bytes 3076
  278.6 4.5 %copy-start.30 = (bf16[256,1024]{1,0:T(8,128)(2,1)S(1)}, bf16[256,1024]{1,0:T(8,128)(2,1)}, u32[]{:S(2)}) copy-start(bf16[256,1024]{1,0:T(8,128)(2,1)} %copy-done.29) | copy-start | bytes 1572868
  283.1 4.6 %copy-start.5 = (bf16[256,768]{1,0:T(8,128)(2,1)S(1)}, bf16[256,768]{1,0:T(8,128)(2,1)}, u32[]{:S(2)}) copy-start(bf16[256,768]{1,0:T(8,128)(2,1)} %param.18) | copy-start | bytes 1179652
  283.1 4.6 %copy-start.27 = (bf16[256,1024]{1,0:T(8,128)(2,1)S(1)}, bf16[256,1024]{1,0:T(8,128)(2,1)}, u32[]{:S(2)}) copy-start(bf16[256,1024]{1,0:T(8,128)(2,1)} %get-tuple-element.136) | copy-start | bytes 1572868
  284.9 4.7 %copy-start.25 = (bf16[6,64,256]{2,1,0:T(8,128)(2,1)S(1)}, bf16[6,64,256]{2,1,0:T(8,128)(2,1)}, u32[]{:S(2)}) copy-start(bf16[6,64,256]{2,1,0:T(8,128)(2,1)} %copy-done.24) | copy-start | bytes 589828
  284.9 5.5 %copy-start.45 = (f32[6,256]{1,0:T(8,128)S(1)}, f32[6,256]{1,0:T(8,128)}, u32[]{:S(2)}) copy-start(f32[6,256]{1,0:T(8,128)} %copy-done.44) | copy-start | bytes 18436
  284.9 6.1 %copy-start.9 = (bf16[1280,6,32]{0,2,1:T(8,128)(2,1)S(1)}, bf16[1280,6,32]{0,2,1:T(8,128)(2,1)}, u32[]{:S(2)}) copy-start(bf16[1280,6,32]{0,2,1:T(8,128)(2,1)} %copy-done.8) | copy-start | bytes 1474564
  289.5 5.8 %copy-start.16 = (bf16[256,6,64]{0,2,1:T(8,128)(2,1)S(1)}, bf16[256,6,64]{0,2,1:T(8,128)(2,1)}, u32[]{:S(2)}) copy-start(bf16[256,6,64]{0,2,1:T(8,128)(2,1)} %copy-done.15) | copy-start | bytes 589828
  291.0 5.2 %copy-start.36 = (s32[1280]{0:T(1024)S(1)}, s32[1280]{0:T(1024)}, u32[]{:S(2)}) copy-start(s32[1280]{0:T(1024)} %copy-done.35) | copy-start | bytes 15364
  291.0 5.2 %copy-start.38 = (s32[1280]{0:T(1024)S(1)}, s32[1280]{0:T(1024)}, u32[]{:S(2)}) copy-start(s32[1280]{0:T(1024)} %copy-done.37) | copy-start | bytes 15364
  291.0 5.2 %copy-start.51 = (pred[1280]{0:T(1024)(128)(4,1)S(1)}, pred[1280]{0:T(1024)(128)(4,1)}, u32[]{:S(2)}) copy-start(pred[1280]{0:T(1024)(128)(4,1)} %copy-done.50) | copy-start | bytes 3844
  291.0 5.2 %copy-start.53 = (s32[256]{0:T(256)S(1)}, s32[256]{0:T(256)}, u32[]{:S(2)}) copy-start(s32[256]{0:T(256)} %copy-done.52) | copy-start | bytes 3076
  291.0 5.2 %copy-start.55 = (s32[256]{0:T(256)S(1)}, s32[256]{0:T(256)}, u32[]{:S(2)}) copy-start(s32[256]{0:T(256)} %copy-done.54) | copy-start | bytes 3076
  293.1 5.1 %copy-start.32 = (f32[768]{0:T(1024)S(1)}, f32[768]{0:T(1024)}, u32[]{:S(2)}) copy-start(f32[768]{0:T(1024)} %copy-done.31) | copy-start | bytes 9220
  293.1 5.6 %copy-start.22 = (f32[1280,32]{0,1:T(8,128)S(1)}, f32[1280,32]{0,1:T(8,128)}, u32[]{:S(2)}) copy-start(f32[1280,32]{0,1:T(8,128)} %copy-done.20) | copy-start | bytes 491524
  296.2 5.7 %copy-start.19 = (f32[1280,32]{0,1:T(8,128)S(1)}, f32[1280,32]{0,1:T(8,128)}, u32[]{:S(2)}) copy-start(f32[1280,32]{0,1:T(8,128)} %copy-done.17) | copy-start | bytes 491524
  303.1 118.6 %copy-start.56 = (f32[256]{0:T(256)S(1)}, f32[256]{0:T(256)}, u32[]{:S(2)}) copy-start(f32[256]{0:T(256)} %get-tuple-element.154) | copy-start | bytes 3076
  418.8 4.2 copy-start.7
  423.0 2.6 copy-start.23
  (14 other events, 22.6 us)
